TPU v7x, 128 devices: a whole 4x4x4 slice. The times are simulated.
128 devices in a mesh: ctx: 16 (over y, x_hi, core), tp: 8 (over z, x_lo).
Axes of the slice: x: 4 (x_hi: 2, x_lo: 2; x = x_hi * 2 + x_lo), y: 4, z: 4, core: 2. Of those that a mesh axis runs over, the one named last changes fastest.
Arguments:
- query_gate: bfloat16 [4096, 16384], P('tp', 'ctx'), may hold values from -6 to 6
- key_gate: bfloat16 [4096, 16384], P('tp', 'ctx'), may hold values from -6 to 6
- value_in: bfloat16 [4096, 16384], P('tp', 'ctx'), may hold values from -6 to 6
- grad_out: bfloat16 [4096, 16384], P('tp', 'ctx'), may hold values from -6 to 6
- skip_bias: float32 [4096], P('tp'), may hold values from -1 to 1
- decay: float32 [256], P('tp'), may hold values from 6.1035156e-06 to 0.0333333333
- w_first: float32 [33, 64], replicated, may hold values from -1 to 1
- b_first: float32 [64], replicated, may hold values from -3.140625 to 3.140625
- w_second: float32 [64, 64], replicated, may hold values from -0.75 to 0.75
- b_second: float32 [64], replicated, may hold values from -3.140625 to 3.140625
- w_third: float32 [64, 256], replicated, may hold values from -0.75 to 0.75
Outputs:
- mixed_out: bfloat16 [4096, 16384], P('tp', 'ctx')
- grad_query: bfloat16 [4096, 16384], P('tp', 'ctx')
- grad_key: bfloat16 [4096, 16384], P('tp', 'ctx')
- grad_value: bfloat16 [4096, 16384], P('tp', 'ctx')
- grad_w_first: float32 [33, 64], replicated
- grad_b_first: float32 [64], replicated
- grad_w_second: float32 [64, 64], replicated
- grad_b_second: float32 [64], replicated
- grad_w_third: float32 [64, 256], replicated
All inputs are finite; a program needn't handle non-finite values.
Results may differ from a plain program's by a relative error of at most 0.0064.
Values may be sent and summed in bfloat16 or wider, within the bound.
A program may use at most 128 MiB of HBM per device.

v0:
```python
import math

import jax
import jax.numpy as jnp
from jax import lax
from jax.sharding import PartitionSpec as P

GSIZE = 16
BANDS = 16


HIGHEST_MODE = lax.Precision.HIGHEST
TRANSFORM_MODE = lax.Precision.HIGH


def wrapped_index(positions, multipliers, modulus):
    upper_part = multipliers // 256
    lower_part = multipliers % 256
    partial_term = positions * upper_part % modulus
    return (partial_term * 256 + positions * lower_part) % modulus


def position_features(start, count, seq_len, band_count):
    positions = start + lax.broadcasted_iota(jnp.int32, (count, 1), 0)
    multipliers = jnp.array(
        [1 + 3 * seq_len // (8 * 2**band_idx) for band_idx in range(band_count)], dtype=jnp.int32
    )[None, :]
    phases = wrapped_index(positions, multipliers, seq_len).astype(jnp.float32) * (
        2.0 * math.pi / seq_len
    )
    ramp_col = positions.astype(jnp.float32) / seq_len
    return (
        jnp.concatenate([ramp_col, jnp.cos(phases), jnp.sin(phases)], axis=1),
        positions.astype(jnp.float32),
    )


def filter_values(features, positions_f, seq_len, decay, w_one, b_one, w_two, b_two, w_three):
    hid_one = jnp.sin(
        jnp.dot(features, w_one, precision=HIGHEST_MODE, preferred_element_type=jnp.float32) + b_one
    )
    hid_two = jnp.sin(
        jnp.dot(hid_one, w_two, precision=HIGHEST_MODE, preferred_element_type=jnp.float32) + b_two
    )
    raw_vals = jnp.dot(hid_two, w_three, precision=HIGHEST_MODE, preferred_element_type=jnp.float32)
    envelope = (
        jnp.exp(-positions_f * decay[None, :]) * jnp.sqrt(2.0 * decay + 1.0 / seq_len)[None, :]
    )
    return jnp.transpose(raw_vals * envelope)


def make_table(row_count, col_count, modulus):
    product = (
        lax.broadcasted_iota(jnp.int32, (row_count, col_count), 0)
        * lax.broadcasted_iota(jnp.int32, (row_count, col_count), 1)
        % modulus
    )
    angles = product.astype(jnp.float32) * (-2.0 * math.pi / modulus)
    return (jnp.cos(angles), jnp.sin(angles))


def dft_tables(fft_len):
    inner_len = 128
    outer_len = fft_len // inner_len
    return (
        make_table(outer_len, outer_len, outer_len)
        + make_table(outer_len, inner_len, fft_len)
        + make_table(inner_len, inner_len, inner_len)
    )


def contract(form, left, right):
    return jnp.einsum(
        form, left, right, precision=TRANSFORM_MODE, preferred_element_type=jnp.float32
    )


def forward_spectrum(signal_f, tables):
    outer_re, outer_im, twist_re, twist_im, inner_re, inner_im = tables
    half_rows = outer_re.shape[0] // 2
    blocks = signal_f.reshape(signal_f.shape[0], half_rows, inner_re.shape[0])
    first_re = contract("kn,cnp->ckp", outer_re[:, :half_rows], blocks)
    first_im = contract("kn,cnp->ckp", outer_im[:, :half_rows], blocks)
    middle_re = first_re * twist_re - first_im * twist_im
    middle_im = first_re * twist_im + first_im * twist_re
    spec_re = contract("ckn,nm->ckm", middle_re, inner_re) - contract(
        "ckn,nm->ckm", middle_im, inner_im
    )
    spec_im = contract("ckn,nm->ckm", middle_re, inner_im) + contract(
        "ckn,nm->ckm", middle_im, inner_re
    )
    return (spec_re, spec_im)


def inverse_signal(spec_re, spec_im, tables):
    outer_re, outer_im, twist_re, twist_im, inner_re, inner_im = tables
    half_rows = outer_re.shape[0] // 2
    fft_len = outer_re.shape[0] * inner_re.shape[0]
    back_re = contract("ckn,nm->ckm", spec_re, inner_re) + contract(
        "ckn,nm->ckm", spec_im, inner_im
    )
    back_im = contract("ckn,nm->ckm", spec_im, inner_re) - contract(
        "ckn,nm->ckm", spec_re, inner_im
    )
    turned_re = back_re * twist_re + back_im * twist_im
    turned_im = back_im * twist_re - back_re * twist_im
    rows_out = contract("nk,ckp->cnp", outer_re[:half_rows], turned_re) + contract(
        "nk,ckp->cnp", outer_im[:half_rows], turned_im
    )
    return rows_out.reshape(rows_out.shape[0], -1) / fft_len


def by_group(spectrum, group_count):
    return spectrum.reshape((group_count, -1) + spectrum.shape[1:])


def owner_forward(signal_bf, filter_bf, bias_own, tables):
    signal_f = lax.optimization_barrier(signal_bf).astype(jnp.float32)
    signal_re, signal_im = forward_spectrum(signal_f, tables)
    filt_re, filt_im = forward_spectrum(filter_bf.astype(jnp.float32), tables)
    group_count = filt_re.shape[0]
    shaped_re = by_group(signal_re, group_count)
    shaped_im = by_group(signal_im, group_count)
    prod_re = shaped_re * filt_re[:, None] - shaped_im * filt_im[:, None]
    prod_im = shaped_re * filt_im[:, None] + shaped_im * filt_re[:, None]
    conv_part = inverse_signal(
        prod_re.reshape(signal_re.shape), prod_im.reshape(signal_re.shape), tables
    )
    inner_bf = (conv_part + bias_own[:, None] * signal_f).astype(jnp.bfloat16)
    return (inner_bf, (signal_re, signal_im, filt_re, filt_im))


def owner_backward(grad_inner_bf, saved, bias_own, tables):
    signal_re, signal_im, filt_re, filt_im = saved
    grad_f = lax.optimization_barrier(grad_inner_bf).astype(jnp.float32)
    grad_re, grad_im = forward_spectrum(grad_f, tables)
    group_count = filt_re.shape[0]
    shaped_gre = by_group(grad_re, group_count)
    shaped_gim = by_group(grad_im, group_count)
    shaped_sre = by_group(signal_re, group_count)
    shaped_sim = by_group(signal_im, group_count)
    back_re = shaped_gre * filt_re[:, None] + shaped_gim * filt_im[:, None]
    back_im = shaped_gim * filt_re[:, None] - shaped_gre * filt_im[:, None]
    back_part = inverse_signal(
        back_re.reshape(grad_re.shape), back_im.reshape(grad_re.shape), tables
    )
    signal_grad = (back_part + bias_own[:, None] * grad_f).astype(jnp.bfloat16)
    corr_re = jnp.sum(shaped_gre * shaped_sre + shaped_gim * shaped_sim, axis=1)
    corr_im = jnp.sum(shaped_gim * shaped_sre - shaped_gre * shaped_sim, axis=1)
    filter_grad = inverse_signal(corr_re, corr_im, tables).astype(jnp.bfloat16)
    return (signal_grad, filter_grad)


def on_device(
    query_gate,
    key_gate,
    value_in,
    grad_out,
    skip_bias,
    decay,
    w_first,
    b_first,
    w_second,
    b_second,
    w_third,
):
    ctx_count = lax.axis_size("ctx")
    ctx_pos = lax.axis_index("ctx")
    tp_pos = lax.axis_index("tp")
    tok_count = query_gate.shape[1]
    seq_len = tok_count * ctx_count
    group_local = decay.shape[0]
    own_channels = query_gate.shape[0] // ctx_count
    features, positions_f = position_features(ctx_pos * tok_count, tok_count, seq_len, BANDS)
    w_cols = lax.dynamic_slice_in_dim(w_third, tp_pos * group_local, group_local, 1)

    def make_filters(w_one, b_one, w_two, b_two, w_three):
        return filter_values(
            features, positions_f, seq_len, decay, w_one, b_one, w_two, b_two, w_three
        )

    filter_f, pullback = jax.vjp(make_filters, w_first, b_first, w_second, b_second, w_cols)
    filter_bf = filter_f.astype(jnp.bfloat16)
    tables = dft_tables(2 * seq_len)
    bias_own = lax.dynamic_slice_in_dim(skip_bias, ctx_pos * own_channels, own_channels, 0)
    query_own, key_own, value_own, cot_own, filter_own = (
        lax.all_to_all(query_gate, "ctx", split_axis=0, concat_axis=1, tiled=True),
        lax.all_to_all(key_gate, "ctx", split_axis=0, concat_axis=1, tiled=True),
        lax.all_to_all(value_in, "ctx", split_axis=0, concat_axis=1, tiled=True),
        lax.all_to_all(grad_out, "ctx", split_axis=0, concat_axis=1, tiled=True),
        lax.all_to_all(filter_bf, "ctx", split_axis=0, concat_axis=1, tiled=True),
    )
    key_f = key_own.astype(jnp.float32)
    value_f = value_own.astype(jnp.float32)
    query_f = query_own.astype(jnp.float32)
    cot_f = cot_own.astype(jnp.float32)
    signal_bf = (key_f * value_f).astype(jnp.bfloat16)
    inner_bf, saved = owner_forward(signal_bf, filter_own, bias_own, tables)
    inner_f = lax.optimization_barrier(inner_bf).astype(jnp.float32)
    mixed_own = (query_f * inner_f).astype(jnp.bfloat16)
    query_grad_own = (cot_f * inner_f).astype(jnp.bfloat16)
    grad_inner_bf = (cot_f * query_f).astype(jnp.bfloat16)
    signal_grad, filter_grad = owner_backward(grad_inner_bf, saved, bias_own, tables)
    signal_grad_f = lax.optimization_barrier(signal_grad).astype(jnp.float32)
    key_grad_own = (signal_grad_f * value_f).astype(jnp.bfloat16)
    value_grad_own = (signal_grad_f * key_f).astype(jnp.bfloat16)
    mixed_out, grad_query, grad_key, grad_value, filter_cot = (
        lax.all_to_all(mixed_own, "ctx", split_axis=1, concat_axis=0, tiled=True),
        lax.all_to_all(query_grad_own, "ctx", split_axis=1, concat_axis=0, tiled=True),
        lax.all_to_all(key_grad_own, "ctx", split_axis=1, concat_axis=0, tiled=True),
        lax.all_to_all(value_grad_own, "ctx", split_axis=1, concat_axis=0, tiled=True),
        lax.all_to_all(filter_grad, "ctx", split_axis=1, concat_axis=0, tiled=True),
    )
    cot_scaled = filter_cot.astype(jnp.float32) * (1.0 / math.sqrt(GSIZE * seq_len))
    grad_one, bias_one, grad_two, bias_two, grad_cols = pullback(cot_scaled)
    grad_three = lax.dynamic_update_slice(
        jnp.zeros(w_third.shape, jnp.float32), grad_cols, (0, tp_pos * group_local)
    )
    summed = lax.psum((grad_one, bias_one, grad_two, bias_two, grad_three), ("ctx", "tp"))
    return (
        mixed_out,
        grad_query,
        grad_key,
        grad_value,
        summed[0],
        summed[1],
        summed[2],
        summed[3],
        summed[4],
    )


def solution(mesh):
    placed = (
        P("tp", "ctx"),
        P("tp", "ctx"),
        P("tp", "ctx"),
        P("tp", "ctx"),
        P("tp"),
        P("tp"),
        P(),
        P(),
        P(),
        P(),
        P(),
    )
    return jax.shard_map(
        on_device,
        mesh=mesh,
        in_specs=placed,
        out_specs=(
            P("tp", "ctx"),
            P("tp", "ctx"),
            P("tp", "ctx"),
            P("tp", "ctx"),
            P(),
            P(),
            P(),
            P(),
            P(),
        ),
        check_vma=False,
    )
```

profile of v0, /device:TPU:1, one launch (start us, length us, event | category | flops | bytes accessed | tf_op | source)
XLA Modules:
  0.0 453.2 jit_solution(8022184324251889778)
XLA Ops:
  16.8 15.6 %all_to_all.154 = bf16[16,2,1024]{2,1,0:T(2,128)(2,1)S(1)} all-to-all(bf16[16,2,1024]{2,1,0:T(2,128)(2,1)S(1)} %all_to_all.122), channel_id=1, replica_groups=mesh['ctx'=16,'tp'=8] {'ctx'}, dimensions={0} | all-to-all | bytes 131072 | tf_op jit(solution)/shard_map/all_to_all | solution.py:191
  40.7 12.8 %all-to-all-done = bf16[16,32,1024]{2,1,0:T(8,128)(2,1)S(1)} async-done(((bf16[16,32,1024]{2,1,0:T(8,128)(2,1)}), bf16[16,32,1024]{2,1,0:T(8,128)(2,1)S(1)}, u32[]{:S(2)}, u32[]{:S(2)}) %all-to-all-start) | async-done | bytes 1048608 | tf_op jit(solution)/shard_map/all_to_all | solution.py:187
  53.5 4.4 all-to-all-start.5
  61.6 13.6 %all-to-all-done.5 = bf16[16,32,1024]{2,1,0:T(8,128)(2,1)S(1)} async-done(((bf16[16,32,1024]{2,1,0:T(8,128)(2,1)}), bf16[16,32,1024]{2,1,0:T(8,128)(2,1)S(1)}, u32[]{:S(2)}, u32[]{:S(2)}) %all-to-all-start.5) | async-done | bytes 1048608 | tf_op jit(solution)/shard_map/all_to_all | solution.py:190
  75.2 5.3 %all-to-all-start.1 = ((bf16[16,32,1024]{2,1,0:T(8,128)(2,1)}), bf16[16,32,1024]{2,1,0:T(8,128)(2,1)}, u32[]{:S(2)}, u32[]{:S(2)}) async-start(bf16[16,32,1024]{2,1,0:T(8,128)(2,1)} %bitcast.291), calls=%async_computation.1 | async-start | bytes 2097152 | tf_op jit(solution)/shard_map/all_to_all | solution.py:188
  88.6 5.6 %fusion.50 = f32[32,256,128]{2,1,0:T(8,128)} fusion(f32[32,128,256]{2,1,0:T(8,128)S(1)} %fusion.87, f32[32,128,256]{2,1,0:T(8,128)S(1)} %fusion.85, f32[256,128]{0,1:T(8,128)S(1)} %get-tuple-element.36, f32[256,128]{0,1:T(8,128)S(1)} %get-tuple-element.37), kind=kOutput, calls=%fused_computation.82 | convolution fusion | flops 808681472 | bytes 12845056 | tf_op jit(solution)/shard_map/ckn,nm->ckm/dot_general | solution.py:73
  94.2 5.6 %convolution_subtract_fusion.1 = f32[32,256,128]{2,1,0:T(8,128)} fusion(f32[32,256,128]{2,1,0:T(8,128)S(1)} %fusion.52, f32[32,128,256]{2,1,0:T(8,128)S(1)} %fusion.87, f32[32,128,256]{2,1,0:T(8,128)S(1)} %fusion.85, f32[256,128]{0,1:T(8,128)S(1)} %get-tuple-element.36, f32[256,128]{0,1:T(8,128)S(1)} %get-tuple-element.37), kind=kOutput, calls=%fused_computation.51 | convolution fusion | flops 809730048 | bytes 17039360 | tf_op jit(solution)/shard_map/ckn,nm->ckm/dot_general | solution.py:73
  99.8 8.5 %fusion.3 = (f32[32,256,128]{2,1,0:T(8,128)S(1)}, f32[32,256,128]{2,1,0:T(8,128)S(1)}, f32[32,256,128]{2,1,0:T(8,128)}) fusion(f32[32,256,128]{2,1,0:T(8,128)} %convolution_subtract_fusion.1, f32[2,256,128]{2,1,0:T(8,128)} %convolution_add_fusion.5, f32[2,256,128]{2,1,0:T(8,128)} %convolution_subtract_fusion.5, f32[32,256,128]{2,1,0:T(8,128)} %fusion.50, ...), kind=kOutput, calls=%fused_computation.11 | convolution fusion | flops 816021504 | bytes 30146560 | tf_op jit(solution)/shard_map/ckn,nm->ckm/dot_general | solution.py:73
  126.0 7.3 %all-to-all-start.2 = ((bf16[16,32,1024]{2,1,0:T(8,128)(2,1)}), bf16[16,32,1024]{2,1,0:T(8,128)(2,1)}, u32[]{:S(2)}, u32[]{:S(2)}) async-start(bf16[16,32,1024]{2,1,0:T(8,128)(2,1)} %bitcast.292), calls=%async_computation.2 | async-start | bytes 2097152 | tf_op jit(solution)/shard_map/all_to_all | solution.py:189
  140.0 10.6 %all-to-all-done.2 = bf16[16,32,1024]{2,1,0:T(8,128)(2,1)} async-done(((bf16[16,32,1024]{2,1,0:T(8,128)(2,1)}), bf16[16,32,1024]{2,1,0:T(8,128)(2,1)}, u32[]{:S(2)}, u32[]{:S(2)}) %all-to-all-start.2) | async-done | bytes 1048608 | tf_op jit(solution)/shard_map/all_to_all | solution.py:189
  157.4 5.7 %fusion.44 = f32[32,256,128]{2,1,0:T(8,128)} fusion(f32[32,128,256]{2,1,0:T(8,128)S(1)} %fusion.88, f32[32,128,256]{2,1,0:T(8,128)S(1)} %fusion.86, f32[256,128]{0,1:T(8,128)S(1)} %get-tuple-element.36, f32[256,128]{0,1:T(8,128)S(1)} %get-tuple-element.37), kind=kOutput, calls=%fused_computation.80 | convolution fusion | flops 808681472 | bytes 12845056 | tf_op jit(solution)/shard_map/ckn,nm->ckm/dot_general | solution.py:73
  171.0 9.2 %fusion.1 = (f32[32,256,128]{2,1,0:T(8,128)}, f32[32,256,128]{2,1,0:T(8,128)}, f32[32,256,128]{2,1,0:T(8,128)}) fusion(f32[32,256,128]{2,1,0:T(8,128)S(1)} %convolution_subtract_fusion.3, f32[2,256,128]{2,1,0:T(8,128)} %convolution_add_fusion.5, f32[2,256,128]{2,1,0:T(8,128)} %convolution_subtract_fusion.5, f32[32,256,128]{2,1,0:T(8,128)} %fusion.44, ...), kind=kOutput, calls=%fused_computation.9 | convolution fusion | flops 816021504 | bytes 30146560 | tf_op jit(solution)/shard_map/ckn,nm->ckm/dot_general | solution.py:73
  180.2 4.4 bitcast_reduce_fusion.1
  192.7 5.0 %all-to-all-start.9 = ((bf16[2,16,1024]{2,0,1:T(2,128)(2,1)}), bf16[2,16,1024]{2,0,1:T(2,128)(2,1)}, u32[]{:S(2)}, u32[]{:S(2)}) async-start(bf16[2,16,1024]{2,0,1:T(2,128)(2,1)} %copy.172), calls=%async_computation.9 | async-start | bytes 131072 | tf_op jit(solution)/shard_map/all_to_all | solution.py:212
  197.6 4.4 fusion.121
  221.3 7.3 %all-to-all-start.4 = ((bf16[32,16,1024]{2,0,1:T(8,128)(2,1)}), bf16[32,16,1024]{2,0,1:T(8,128)(2,1)S(1)}, u32[]{:S(2)}, u32[]{:S(2)}) async-start(bf16[32,16,1024]{2,0,1:T(8,128)(2,1)} %bitcast.264), calls=%async_computation.4 | async-start | bytes 2097152 | tf_op jit(solution)/shard_map/all_to_all | solution.py:208
  229.6 16.1 %all-to-all-done.4 = bf16[32,16,1024]{2,0,1:T(8,128)(2,1)S(1)} async-done(((bf16[32,16,1024]{2,0,1:T(8,128)(2,1)}), bf16[32,16,1024]{2,0,1:T(8,128)(2,1)S(1)}, u32[]{:S(2)}, u32[]{:S(2)}) %all-to-all-start.4) | async-done | bytes 1048608 | tf_op jit(solution)/shard_map/all_to_all | solution.py:208
  245.8 4.4 all-to-all-start.6
  252.4 15.0 %all-to-all-done.6 = bf16[32,16,1024]{2,0,1:T(8,128)(2,1)S(1)} async-done(((bf16[32,16,1024]{2,0,1:T(8,128)(2,1)}), bf16[32,16,1024]{2,0,1:T(8,128)(2,1)S(1)}, u32[]{:S(2)}, u32[]{:S(2)}) %all-to-all-start.6) | async-done | bytes 1048608 | tf_op jit(solution)/shard_map/all_to_all | solution.py:209
  267.4 4.4 all-to-all-start.7
  277.2 11.8 %all-to-all-done.7 = bf16[32,16,1024]{2,0,1:T(8,128)(2,1)S(1)} async-done(((bf16[32,16,1024]{2,0,1:T(8,128)(2,1)}), bf16[32,16,1024]{2,0,1:T(8,128)(2,1)S(1)}, u32[]{:S(2)}, u32[]{:S(2)}) %all-to-all-start.7) | async-done | bytes 1048608 | tf_op jit(solution)/shard_map/all_to_all | solution.py:210
  289.1 5.0 %all-to-all-start.8 = ((bf16[32,16,1024]{2,0,1:T(8,128)(2,1)}), bf16[32,16,1024]{2,0,1:T(8,128)(2,1)}, u32[]{:S(2)}, u32[]{:S(2)}) async-start(bf16[32,16,1024]{2,0,1:T(8,128)(2,1)} %bitcast.284), calls=%async_computation.8 | async-start | bytes 2097152 | tf_op jit(solution)/shard_map/all_to_all | solution.py:211
  305.5 69.4 %all-reduce = (f32[33,64]{1,0:T(8,128)}, f32[64]{0:T(128)}, f32[64,64]{1,0:T(8,128)}, f32[64]{0:T(128)}) all-reduce(f32[33,64]{1,0:T(8,128)S(1)} %fusion.83, f32[64]{0:T(128)S(1)} %get-tuple-element.32, f32[64,64]{1,0:T(8,128)} %fusion.275, f32[64]{0:T(128)} %get-tuple-element.34), channel_id=1, replica_groups=mesh['ctx'=16,'tp'=8] {'ctx','tp'}, use_global_device_ids=true, to_apply=%region_2.3 | all-reduce | flops 6336 | bytes 50688 | tf_op jit(solution)/shard_map/psum | solution.py:219
  374.8 65.3 %all-reduce.3.cloned.1.call-done = f32[64,256]{1,0:T(8,128)} async-done(((f32[64,256]{1,0:T(8,128)}), f32[64,256]{1,0:T(8,128)}) %all-reduce.3.cloned.1.call-update) | async-done | bytes 65552 | tf_op jit(solution)/shard_map/psum | solution.py:219
  (133 shorter events, 121.7 us)
Async XLA Ops:
  7.2 8.5 %copy-start = (f32[64,256]{1,0:T(8,128)S(1)}, f32[64,256]{1,0:T(8,128)}, u32[]{:S(2)}) copy-start(f32[64,256]{1,0:T(8,128)} %param.22) | copy-start | bytes 196612
  9.0 2.7 copy-start.19
  32.3 21.2 %all-to-all-start = ((bf16[16,32,1024]{2,1,0:T(8,128)(2,1)}), bf16[16,32,1024]{2,1,0:T(8,128)(2,1)S(1)}, u32[]{:S(2)}, u32[]{:S(2)}) async-start(bf16[16,32,1024]{2,1,0:T(8,128)(2,1)} %bitcast.289), calls=%async_computation | async-start | bytes 2097152 | tf_op jit(solution)/shard_map/all_to_all | solution.py:187
  37.2 2.4 copy-start.7
  39.0 22.1 %copy-start.11 = (f32[256,256]{1,0:T(8,128)}, f32[256,256]{1,0:T(8,128)S(1)}, u32[]{:S(2)}) copy-start(f32[256,256]{1,0:T(8,128)S(1)} %fusion.81) | copy-start | bytes 786436
  53.5 21.7 %all-to-all-start.5 = ((bf16[16,32,1024]{2,1,0:T(8,128)(2,1)}), bf16[16,32,1024]{2,1,0:T(8,128)(2,1)S(1)}, u32[]{:S(2)}, u32[]{:S(2)}) async-start(bf16[16,32,1024]{2,1,0:T(8,128)(2,1)} %bitcast.290), calls=%async_computation.5 | async-start | bytes 2097152 | tf_op jit(solution)/shard_map/all_to_all | solution.py:190
  75.2 50.8 %all-to-all-start.1 = ((bf16[16,32,1024]{2,1,0:T(8,128)(2,1)}), bf16[16,32,1024]{2,1,0:T(8,128)(2,1)}, u32[]{:S(2)}, u32[]{:S(2)}) async-start(bf16[16,32,1024]{2,1,0:T(8,128)(2,1)} %bitcast.291), calls=%async_computation.1 | async-start | bytes 2097152 | tf_op jit(solution)/shard_map/all_to_all | solution.py:188
  81.0 2.4 copy-start.4
  126.0 24.6 %all-to-all-start.2 = ((bf16[16,32,1024]{2,1,0:T(8,128)(2,1)}), bf16[16,32,1024]{2,1,0:T(8,128)(2,1)}, u32[]{:S(2)}, u32[]{:S(2)}) async-start(bf16[16,32,1024]{2,1,0:T(8,128)(2,1)} %bitcast.292), calls=%async_computation.2 | async-start | bytes 2097152 | tf_op jit(solution)/shard_map/all_to_all | solution.py:189
  150.6 2.2 copy-start.15
  171.0 9.2 %copy-start.3 = (f32[32,256,128]{2,1,0:T(8,128)S(1)}, f32[32,256,128]{2,1,0:T(8,128)}, u32[]{:S(2)}) copy-start(f32[32,256,128]{2,1,0:T(8,128)} %convolution_subtract_fusion.1) | copy-start | bytes 12582916
  192.7 28.6 %all-to-all-start.9 = ((bf16[2,16,1024]{2,0,1:T(2,128)(2,1)}), bf16[2,16,1024]{2,0,1:T(2,128)(2,1)}, u32[]{:S(2)}, u32[]{:S(2)}) async-start(bf16[2,16,1024]{2,0,1:T(2,128)(2,1)} %copy.172), calls=%async_computation.9 | async-start | bytes 131072 | tf_op jit(solution)/shard_map/all_to_all | solution.py:212
  197.6 4.4 copy-start.2
  204.1 2.2 copy-start.1
  206.3 2.1 copy-start.10
  216.9 3.0 copy-start.5
  221.3 24.5 %all-to-all-start.4 = ((bf16[32,16,1024]{2,0,1:T(8,128)(2,1)}), bf16[32,16,1024]{2,0,1:T(8,128)(2,1)S(1)}, u32[]{:S(2)}, u32[]{:S(2)}) async-start(bf16[32,16,1024]{2,0,1:T(8,128)(2,1)} %bitcast.264), calls=%async_computation.4 | async-start | bytes 2097152 | tf_op jit(solution)/shard_map/all_to_all | solution.py:208
  245.8 21.6 %all-to-all-start.6 = ((bf16[32,16,1024]{2,0,1:T(8,128)(2,1)}), bf16[32,16,1024]{2,0,1:T(8,128)(2,1)S(1)}, u32[]{:S(2)}, u32[]{:S(2)}) async-start(bf16[32,16,1024]{2,0,1:T(8,128)(2,1)} %bitcast.286), calls=%async_computation.6 | async-start | bytes 2097152 | tf_op jit(solution)/shard_map/all_to_all | solution.py:209
  250.1 44.0 %copy-start.21 = (f32[32]{0:T(128)S(1)}, f32[32]{0:T(128)}, u32[]{:S(2)}) copy-start(f32[32]{0:T(128)} %param.17) | copy-start | bytes 388
  252.4 48.7 %copy-start.17 = (f32[1024,64]{0,1:T(8,128)S(1)}, f32[1024,64]{0,1:T(8,128)}, u32[]{:S(2)}) copy-start(f32[1024,64]{0,1:T(8,128)} %copy-done.16) | copy-start | bytes 786436
  267.4 21.7 %all-to-all-start.7 = ((bf16[32,16,1024]{2,0,1:T(8,128)(2,1)}), bf16[32,16,1024]{2,0,1:T(8,128)(2,1)S(1)}, u32[]{:S(2)}, u32[]{:S(2)}) async-start(bf16[32,16,1024]{2,0,1:T(8,128)(2,1)} %bitcast.285), calls=%async_computation.7 | async-start | bytes 2097152 | tf_op jit(solution)/shard_map/all_to_all | solution.py:210
  289.1 85.8 %all-to-all-start.8 = ((bf16[32,16,1024]{2,0,1:T(8,128)(2,1)}), bf16[32,16,1024]{2,0,1:T(8,128)(2,1)}, u32[]{:S(2)}, u32[]{:S(2)}) async-start(bf16[32,16,1024]{2,0,1:T(8,128)(2,1)} %bitcast.284), calls=%async_computation.8 | async-start | bytes 2097152 | tf_op jit(solution)/shard_map/all_to_all | solution.py:211
  294.0 146.1 %all-reduce.3.cloned.1.call-start = ((), (), s32[]{:S(2)}) async-start(), calls=%async_computation.10 | async-start | bytes 131072 | tf_op jit(solution)/shard_map/psum | solution.py:219
  440.1 5.2 %copy-start.20 = (f32[64,256]{1,0:T(8,128)S(1)}, f32[64,256]{1,0:T(8,128)}, u32[]{:S(2)}) copy-start(f32[64,256]{1,0:T(8,128)} %all-reduce.3.cloned.1.call-done) | copy-start | bytes 196612
  (8 other events, 12.1 us)
Sparse Core Ops, SparseCore 0:
  300.2 139.9 all-reduce.2
where the time goes:
time: 462 us; the launch traced here: 453 us
  waiting for transfers between devices  145 us (31%)
  matrix products  106 us (23%)
  blocking collectives  84.9 us (18%)
  starting transfers between devices  46.8 us (10%)
  local copies, waits for them, and re-layouts  32.6 us (7%)
  other arithmetic  22.8 us (5%)
  between operations  15.1 us (3%)
    dot_general x36, matrix products, contract(): jnp.einsum(form, left, right, precision=TRANSFORM_MODE, preferred_element...  90.2 us
    psum x1, blocking collectives, on_device(): lax.psum((grad_one, bias_one, grad_two, bias_two, grad_three), ('ctx', 't...  69.4 us
    psum x1, waiting for transfers between devices, on_device(): lax.psum((grad_one, bias_one, grad_two, bias_two, grad_three), ('ctx', 't...  65.3 us
    all_to_all x1, waiting for transfers between devices, on_device(): lax.all_to_all(mixed_own, 'ctx', split_axis=1, concat_axis=0, tiled=True)  16.1 us
    all_to_all x1, blocking collectives, on_device(): lax.all_to_all(filter_bf, 'ctx', split_axis=0, concat_axis=1, tiled=True)  15.6 us
    all_to_all x1, waiting for transfers between devices, on_device(): lax.all_to_all(query_grad_own, 'ctx', split_axis=1, concat_axis=0, tiled=...  15 us
    all_to_all x1, waiting for transfers between devices, on_device(): lax.all_to_all(grad_out, 'ctx', split_axis=0, concat_axis=1, tiled=True)  13.6 us
    all_to_all x1, waiting for transfers between devices, on_device(): lax.all_to_all(query_gate, 'ctx', split_axis=0, concat_axis=1, tiled=True)  12.8 us
  transfers between devices with their start and end apart: 10, of which 7 were waited for; matrix products, arithmetic and copies ran while one was open for 23% of the time, Pallas kernels for 0%

commit v1 on v0

v1 whole, which is shorter than its diff:
```python
import functools
import math

import jax
import jax.numpy as jnp
import ml_dtypes
import numpy as np
from jax import lax
from jax.experimental import pallas as pl
from jax.experimental.pallas import tpu as pltpu
from jax.sharding import PartitionSpec as P

MESH = pl.DeviceIdType.MESH
F32 = jnp.float32
BF16 = jnp.bfloat16
HIGHEST = lax.Precision.HIGHEST

SEQ = 16384
FFT = 2 * SEQ
GSIZE = 16
BANDS = 16
EMB = 2 * BANDS + 1
ORDER = 64
CTX = 16
TP = 8
TOK = SEQ // CTX
CHL = 512
GRL = 32
OWN = CHL // CTX
FROWS = 40
ANY = pl.BlockSpec(memory_space=pl.ANY)
VMEM = pl.BlockSpec(memory_space=pltpu.VMEM)
SMEM = pl.BlockSpec(memory_space=pltpu.SMEM)

PI_A = 3.140625
PI_B = float(np.float32(math.floor((math.pi - PI_A) * 2.0**22) / 2.0**22))
PI_C = math.pi - PI_A - PI_B


def halves(table):
    high = table.astype(ml_dtypes.bfloat16)
    low = (table - high.astype(np.float64)).astype(ml_dtypes.bfloat16)
    return [high, low]


@functools.cache
def tables():
    k1 = np.arange(256)
    n1 = np.arange(128)
    n2 = np.arange(128)
    outer = 2.0 * np.pi * (np.outer(k1, n1) % 256) / 256.0
    cos1, sin1 = np.cos(outer), np.sin(outer)
    by_rows = lambda first, second: np.stack(
        [first.reshape(256, 16, 8), second.reshape(256, 16, 8)], axis=2
    ).reshape(256, 256)
    fwd = np.concatenate([by_rows(cos1, sin1), by_rows(-sin1, cos1)], axis=0)
    inv = np.concatenate([by_rows(cos1, sin1).T, by_rows(-sin1, cos1).T], axis=1) / FFT
    fwd_real = np.concatenate([cos1, -sin1], axis=0)
    inv_real = np.concatenate([cos1.T, -sin1.T], axis=1) / FFT
    inner = 2.0 * np.pi * (np.outer(n2, n2) % 128) / 128.0
    cos2, sin2 = np.cos(inner), np.sin(inner)
    mid_fwd = np.block([[cos2, -sin2], [sin2, cos2]])
    mid_inv = np.block([[cos2, sin2], [-sin2, cos2]])
    turn = 2.0 * np.pi * np.outer(k1, n2) / FFT
    twiddle = np.concatenate([np.cos(turn), -np.sin(turn)], axis=0).astype(np.float32)
    wide = np.concatenate(halves(fwd) + halves(mid_fwd) + halves(mid_inv), axis=0)
    thin = np.concatenate(halves(fwd_real), axis=0)
    long = np.concatenate(halves(inv) + halves(inv_real), axis=0)
    t = np.arange(SEQ, dtype=np.int64)
    steps = np.array([1 + 3 * SEQ // (8 * 2**b) for b in range(BANDS)], dtype=np.int64)
    phase = 2.0 * np.pi * (np.outer(steps, t) % SEQ) / SEQ
    features = np.zeros((FROWS, SEQ), np.float32)
    features[0] = t / SEQ
    features[1 : 1 + BANDS] = np.cos(phase)
    features[1 + BANDS : EMB] = np.sin(phase)
    features[EMB] = 1.0
    return wide, thin, long, twiddle, features


def dot(left, right):
    return jnp.dot(left, right, preferred_element_type=F32)


def dot_full(left, right, dims):
    return lax.dot_general(
        left, right, (dims, ((), ())), precision=HIGHEST, preferred_element_type=F32
    )


def split(x):
    high = x.astype(BF16)
    return high, (x - high.astype(F32)).astype(BF16)


def sin_cos(x):
    turns = jnp.floor(x * (1.0 / math.pi) + 0.5)
    r = ((x - turns * PI_A) - turns * PI_B) - turns * PI_C
    flip = 1.0 - 2.0 * (turns - 2.0 * jnp.floor(turns * 0.5))
    z = r * r
    sine, cosine = 0.0, 0.0
    for i in range(6, -1, -1):
        sine = sine * z + (-1.0) ** i / math.factorial(2 * i + 1)
        cosine = cosine * z + (-1.0) ** i / math.factorial(2 * i)
    return sine * r * flip, cosine * flip


def rows_to_tiles(x):
    return jnp.transpose(jnp.stack([x[:, 128 * i : 128 * i + 128] for i in range(8)], axis=0), (1, 0, 2))


def tiles_to_rows(x):
    x = jnp.transpose(x, (1, 0, 2))
    return jnp.concatenate([x[i] for i in range(8)], axis=1)


S_IN, R_IN, L_IN = 0, 4, 8
S_OUT, R_OUT, L_OUT = 12, 16, 20
S_FIL, R_FIL, S_FG, R_FG, S_RS, R_RS, S_TP, R_TP, S_AG, R_AG = range(24, 34)
C_ARG, C_TAB = 34, 38
N_SEM = 44


def mixer_kernel(
    query, key, value, cot, skip, decay, w1, b1, w2, b2, w3, wide_h, thin_h, long_h, twid_h, feat_h,
    back, summed,
    q_v, k_v, v_v, g_v, wide, thin, long, twid, feat,
    send, recv, spec_s, spec_g, spec_f, corr, out,
    w1a, w2a, h1a, c1, s2, c2, dec, env, fsend, frecv, gsend, grecv, draw, dact, part, rs, tpx, agx, sem,
):
    me = lax.axis_index("ctx")
    tp = lax.axis_index("tp")

    def ring(step):
        return lax.rem(me + step, CTX)

    def remote(src, dst, s, r, axis, j):
        return pltpu.make_async_remote_copy(
            src_ref=src, dst_ref=dst, send_sem=sem.at[s], recv_sem=sem.at[r], device_id={axis: j}, device_id_type=MESH
        )

    def local(src, dst, s):
        return pltpu.make_async_copy(src, dst, sem.at[s])

    def landed(ref, s):
        pltpu.make_async_copy(ref, ref, sem.at[s]).wait()

    loads = [local(a, b, C_ARG + i) for i, (a, b) in enumerate(((key, k_v), (value, v_v), (query, q_v), (cot, g_v)))]
    for c in loads:
        c.start()
    rest = [
        local(feat_h.at[:, pl.ds(pl.multiple_of(me * TOK, TOK), TOK)], feat.at[pl.ds(0, FROWS)], C_TAB),
        local(wide_h, wide, C_TAB + 1),
        local(thin_h, thin, C_TAB + 2),
        local(long_h, long, C_TAB + 3),
        local(twid_h, twid, C_TAB + 4),
    ]
    for c in rest:
        c.start()

    barrier = pltpu.get_barrier_semaphore()

    @pl.loop(1, CTX)
    def _(step):
        pl.semaphore_signal(barrier, inc=1, device_id={"ctx": ring(step)}, device_id_type=MESH)

    @pl.loop(1, TP)
    def _(step):
        pl.semaphore_signal(barrier, inc=1, device_id={"tp": lax.rem(tp + step, TP)}, device_id_type=MESH)

    def product(left, right, j, kind):
        rows = pl.ds(pl.multiple_of(j * OWN, OWN), OWN)
        x = left[rows, :].astype(F32) * right[rows, :].astype(F32)
        y = rows_to_tiles(x).reshape(16, 16, 128).astype(BF16)
        for p in range(16):
            send[2 * kind + p // 8, j, p % 8 // 2, :, 128 * (p % 2) : 128 * (p % 2) + 128] = y[p]

    def mine(rnd):
        return recv.at[rnd, :, pl.ds(pl.multiple_of(me * 16, 16), 16), :]

    def push(rnd, j):
        remote(send.at[rnd, j], mine(rnd), S_IN + rnd, R_IN + rnd, "ctx", j).start()

    loads[0].wait()
    loads[1].wait()
    product(k_v, v_v, me, 0)
    pl.semaphore_wait(barrier, CTX - 1 + TP - 1)

    @pl.loop(1, CTX)
    def _(step):
        product(k_v, v_v, ring(step), 0)
        push(0, ring(step))

    @pl.loop(1, CTX)
    def _(step):
        push(1, ring(step))

    loads[2].wait()
    loads[3].wait()
    product(q_v, g_v, me, 1)

    @pl.loop(1, CTX)
    def _(step):
        product(q_v, g_v, ring(step), 1)
        push(2, ring(step))

    @pl.loop(1, CTX)
    def _(step):
        push(3, ring(step))

    own = [local(send.at[rnd, me], mine(rnd), L_IN + rnd) for rnd in range(4)]
    for c in own:
        c.start()

    rest[0].wait()
    feat[FROWS:, :] = jnp.zeros((64 - FROWS, TOK), F32)
    w1a[...] = jnp.zeros(w1a.shape, F32)
    w1a[0:EMB, :] = w1[...]
    w1a[EMB : EMB + 1, :] = b1[...]
    w2a[...] = jnp.zeros(w2a.shape, F32)
    w2a[0:ORDER, :] = w2[...]
    w2a[ORDER : ORDER + 1, :] = b2[...]
    h1a[ORDER:, :] = (lax.broadcasted_iota(jnp.int32, (8, TOK), 0) == 0).astype(F32)
    sine, cosine = sin_cos(dot_full(w1a[...], feat[0:FROWS, :], ((0,), (0,))))
    h1a[0:ORDER, :] = sine
    c1[...] = cosine
    sine, cosine = sin_cos(dot_full(w2a[...], h1a[...], ((0,), (0,))))
    s2[...] = sine
    c2[...] = cosine
    w3_own = pltpu.roll(w3[...], lax.rem(TP * GRL - tp * GRL, TP * GRL), 1)[:, 0:GRL]
    raw = dot_full(w3_own, s2[...], ((0,), (0,)))
    dec[...] = jnp.zeros(dec.shape, F32)
    dec[0:1, :] = decay[...]
    rate = dot_full(dec[...], h1a[ORDER:, :], ((0,), (0,)))
    position = (me * TOK + lax.broadcasted_iota(jnp.int32, (GRL, TOK), 1)).astype(F32)
    env[...] = jnp.exp(-position * rate) * jnp.sqrt(2.0 * rate + 1.0 / SEQ)
    tiles = rows_to_tiles((raw * env[...]).astype(BF16).astype(F32))
    for j in range(CTX):
        fsend[j, :, 0:128] = tiles[2 * j]
        fsend[j, :, 128:256] = tiles[2 * j + 1]

    @pl.loop(1, CTX)
    def _(step):
        remote(fsend.at[ring(step)], frecv.at[me], S_FIL, R_FIL, "ctx", ring(step)).start()

    frecv[me] = fsend[me]

    for c in rest[1:]:
        c.wait()
    t_re = lambda: twid[0:256, :]
    t_im = lambda: twid[256:512, :]

    def forward_mid(first, pair):
        re = first[0:256, 128 * pair : 128 * pair + 128]
        im = first[256:512, 128 * pair : 128 * pair + 128]
        high, low = split(jnp.concatenate([re * t_re() - im * t_im(), re * t_im() + im * t_re()], axis=1))
        return dot(high, wide[1024:1280, :]) + dot(high, wide[1280:1536, :]) + dot(low, wide[1024:1280, :])

    def inverse_mid(spectra):
        res, ims = [], []
        for spectrum in spectra:
            high, low = split(spectrum)
            x = dot(high, wide[1536:1792, :]) + dot(high, wide[1792:2048, :]) + dot(low, wide[1536:1792, :])
            re, im = x[:, 0:128], x[:, 128:256]
            res.append(re * t_re() + im * t_im())
            ims.append(im * t_re() - re * t_im())
        return split(jnp.concatenate([jnp.concatenate(res, axis=1), jnp.concatenate(ims, axis=1)], axis=0))

    landed(frecv.at[pl.ds(0, CTX - 1)], R_FIL)
    taps = frecv[...].reshape(128, 256).astype(BF16)
    first = dot(thin[0:512, :], taps) + dot(thin[512:1024, :], taps)
    for g in range(2):
        spec_f[g] = forward_mid(first, g)

    def arrived(rnd):
        own[rnd].wait()
        landed(recv.at[rnd, :, pl.ds(0, 240), :], R_IN + rnd)

    def forward(rnd, d, spec, g):
        x = recv[rnd, d]
        first = dot(wide[0:512, :], x) + dot(wide[512:1024, :], x)
        for pair in range(2):
            spec[g, d, pair] = forward_mid(first, pair)

    in_second = lax.broadcasted_iota(jnp.int32, (256, 128), 0) // 8 % 2 == 1

    def inverse(rnd, d, spec, g, sign):
        spectra = []
        for pair in range(2):
            re, im = spec[g, d, pair, :, 0:128], spec[g, d, pair, :, 128:256]
            f_re, f_im = spec_f[g, :, 0:128], sign * spec_f[g, :, 128:256]
            spectra.append(jnp.concatenate([re * f_re - im * f_im, re * f_im + im * f_re], axis=1))
        high, low = inverse_mid(spectra)
        y = dot(long[0:256, :], high) + dot(long[256:512, :], high) + dot(long[0:256, :], low)
        base = me * OWN + g * 16 + d * 4
        scale = jnp.concatenate(
            [jnp.where(in_second, skip[base + 2 * pair + 1], skip[base + 2 * pair]) for pair in range(2)], axis=1
        )
        out[rnd, d] = (y + scale * recv[rnd, d].astype(F32)).astype(BF16)

    def give(rnd):
        @pl.loop(1, CTX)
        def _(step):
            j = ring(step)
            src = out.at[rnd, :, pl.ds(pl.multiple_of(j * 16, 16), 16), :]
            remote(src, back.at[rnd, me], S_OUT + rnd, R_OUT + rnd, "ctx", j).start()

        keep = local(out.at[rnd, :, pl.ds(pl.multiple_of(me * 16, 16), 16), :], back.at[rnd, me], L_OUT + rnd)
        keep.start()
        return keep

    kept = []
    for g in range(2):
        arrived(g)

        @pl.loop(0, 4)
        def _(d):
            forward(g, d, spec_s, g)
            inverse(g, d, spec_s, g, 1.0)

        kept.append(give(g))

    for g in range(2):
        arrived(2 + g)
        corr[g] = jnp.zeros((256, 256), F32)

        @pl.loop(0, 4)
        def _(d):
            forward(2 + g, d, spec_g, g)
            for pair in range(2):
                s_re, s_im = spec_s[g, d, pair, :, 0:128], spec_s[g, d, pair, :, 128:256]
                g_re, g_im = spec_g[g, d, pair, :, 0:128], spec_g[g, d, pair, :, 128:256]
                corr[g, :, 0:128] += g_re * s_re + g_im * s_im
                corr[g, :, 128:256] += g_im * s_re - g_re * s_im

    high, low = inverse_mid([corr[0], corr[1]])
    taps = dot(long[512:640, :], high) + dot(long[640:768, :], high) + dot(long[512:640, :], low)
    gsend[...] = taps.astype(BF16).astype(F32).reshape(CTX, 8, 256)

    @pl.loop(1, CTX)
    def _(step):
        remote(gsend.at[ring(step)], grecv.at[me], S_FG, R_FG, "ctx", ring(step)).start()

    grecv[me] = gsend[me]

    for g in range(2):

        @pl.loop(0, 4)
        def _(d):
            inverse(2 + g, d, spec_g, g, -1.0)

        kept.append(give(2 + g))

    landed(grecv.at[pl.ds(0, CTX - 1)], R_FG)
    got = jnp.stack([grecv[j, :, 128 * g : 128 * g + 128] for j in range(CTX) for g in range(2)], axis=0)
    draw[0:GRL, :] = tiles_to_rows(got) * (1.0 / math.sqrt(GSIZE * SEQ)) * env[...]
    draw[GRL:, :] = jnp.zeros((128 - GRL, TOK), F32)
    w3_own = pltpu.roll(w3[...], lax.rem(TP * GRL - tp * GRL, TP * GRL), 1)[:, 0:GRL]
    dact[0:ORDER, :] = dot_full(w3_own, draw[0:GRL, :], ((1,), (0,))) * c2[...]
    dact[ORDER:, :] = dot_full(w2[...], dact[0:ORDER, :], ((1,), (0,))) * c1[...]
    g_feat = dot_full(feat[...], dact[...], ((1,), (1,)))
    g_hid = dot_full(h1a[0:ORDER, :], dact[...], ((1,), (1,)))
    g_out = dot_full(s2[...], draw[...], ((1,), (1,)))
    g_out = pltpu.roll(jnp.concatenate([g_out, jnp.zeros((ORDER, 128), F32)], axis=1), tp * GRL, 1)
    for i in range(8):
        part[2 * i, :, 0:128] = g_feat[8 * i : 8 * i + 8, :]
        part[2 * i, :, 128:256] = g_hid[8 * i : 8 * i + 8, :]
        part[2 * i + 1] = g_out[8 * i : 8 * i + 8, :]

    @pl.loop(1, CTX)
    def _(step):
        remote(part.at[ring(step)], rs.at[me], S_RS, R_RS, "ctx", ring(step)).start()

    rs[me] = part[me]
    landed(rs.at[pl.ds(0, CTX - 1)], R_RS)
    tpx[tp] = jnp.sum(rs[...], axis=0)

    @pl.loop(1, TP)
    def _(step):
        remote(tpx.at[tp], tpx.at[tp], S_TP, R_TP, "tp", lax.rem(tp + step, TP)).start()

    landed(tpx.at[pl.ds(0, TP - 1)], R_TP)
    agx[me] = jnp.sum(tpx[...], axis=0)

    @pl.loop(1, CTX)
    def _(step):
        remote(agx.at[me], agx.at[me], S_AG, R_AG, "ctx", ring(step)).start()

    landed(agx.at[pl.ds(0, CTX - 1)], R_AG)
    summed[...] = agx[...]

    for rnd in range(4):
        kept[rnd].wait()
        landed(back.at[rnd, pl.ds(0, CTX - 1)], R_OUT + rnd)
    for rnd in range(4):
        landed(send.at[rnd, pl.ds(0, CTX - 1)], S_IN + rnd)
        landed(out.at[rnd, :, pl.ds(0, 240), :], S_OUT + rnd)
    landed(fsend.at[pl.ds(0, CTX - 1)], S_FIL)
    landed(gsend.at[pl.ds(0, CTX - 1)], S_FG)
    landed(part.at[pl.ds(0, CTX - 1)], S_RS)
    landed(tpx.at[pl.ds(0, TP - 1)], S_TP)
    landed(agx.at[pl.ds(0, CTX - 1)], S_AG)


def gate_kernel(
    query, key, value, cot, back, summed, mixed, g_query, g_key, g_value, o_w1, o_b1, o_w2, o_b2, o_w3
):
    count = query.shape[0] // OWN
    for j in range(count):
        rows = slice(OWN * j, OWN * j + OWN)

        def whole(kind):
            tiles = [
                back[2 * kind + p // 8, j, p % 8 // 2, :, 128 * (p % 2) : 128 * (p % 2) + 128] for p in range(16)
            ]
            return tiles_to_rows(jnp.stack(tiles, axis=0).astype(F32).reshape(OWN, 8, 128))

        inner = whole(0)
        mixed[rows, :] = (query[rows, :].astype(F32) * inner).astype(BF16)
        g_query[rows, :] = (cot[rows, :].astype(F32) * inner).astype(BF16)
        g_signal = whole(1)
        g_key[rows, :] = (g_signal * value[rows, :].astype(F32)).astype(BF16)
        g_value[rows, :] = (g_signal * key[rows, :].astype(F32)).astype(BF16)

    @pl.when(pl.program_id(0) == 0)
    def _():
        feat = jnp.concatenate([summed[2 * i, :, 0:128] for i in range(8)], axis=0)
        turned = pltpu.roll(feat, 64, 1)
        o_w1[...] = turned[0:EMB, 0:ORDER]
        o_b1[...] = turned[EMB : EMB + 1, 0:ORDER]
        o_b2[...] = feat[EMB : EMB + 1, 0:ORDER]
        o_w2[...] = jnp.concatenate([summed[2 * i, :, 128:256] for i in range(8)], axis=0)[:, 0:ORDER]
        o_w3[...] = jnp.concatenate([summed[2 * i + 1] for i in range(8)], axis=0)


def on_device(query, key, value, cot, skip, decay, w1, b1, w2, b2, w3):
    wide, thin, long, twid, feat = (jnp.asarray(t) for t in tables())
    f32 = lambda *shape: pltpu.VMEM(shape, F32)
    b16 = lambda *shape: pltpu.VMEM(shape, BF16)
    back, summed = pl.pallas_call(
        mixer_kernel,
        name="mixer",
        out_shape=(
            jax.ShapeDtypeStruct((4, CTX, 4, 16, 256), BF16),
            jax.ShapeDtypeStruct((CTX, 8, 256), F32),
        ),
        in_specs=[ANY] * 4 + [SMEM] + [VMEM] * 6 + [ANY] * 5,
        out_specs=(ANY, VMEM),
        scratch_shapes=[
            *[b16(CHL, TOK) for _ in range(4)],
            b16(*wide.shape), b16(*thin.shape), b16(*long.shape), f32(*twid.shape), f32(64, TOK),
            b16(4, CTX, 4, 16, 256), b16(4, 4, 256, 256),
            f32(2, 4, 2, 256, 256), f32(2, 4, 2, 256, 256), f32(2, 256, 256), f32(2, 256, 256),
            b16(4, 4, 256, 256),
            f32(FROWS, ORDER), f32(ORDER + 8, ORDER), f32(ORDER + 8, TOK), f32(ORDER, TOK), f32(ORDER, TOK),
            f32(ORDER, TOK), f32(8, GRL), f32(GRL, TOK),
            f32(CTX, 8, 256), f32(CTX, 8, 256), f32(CTX, 8, 256), f32(CTX, 8, 256),
            f32(128, TOK), f32(128, TOK),
            f32(CTX, 8, 256), f32(CTX, 8, 256), f32(TP, 8, 256), f32(CTX, 8, 256),
            pltpu.SemaphoreType.DMA((N_SEM,)),
        ],
        compiler_params=pltpu.CompilerParams(
            collective_id=0, has_side_effects=True, vmem_limit_bytes=56 * 1024 * 1024
        ),
        cost_estimate=pl.CostEstimate(flops=12_000_000_000, bytes_accessed=10_000_000, transcendentals=200_000),
    )(query, key, value, cot, skip, decay[None], w1, b1[None], w2, b2[None], w3, wide, thin, long, twid, feat)
    step = 2
    gates = pl.BlockSpec((OWN * step, TOK), lambda i: (i, 0))
    fixed = lambda *shape: pl.BlockSpec(shape, lambda i: (0,) * len(shape))
    mixed, g_query, g_key, g_value, o_w1, o_b1, o_w2, o_b2, o_w3 = pl.pallas_call(
        gate_kernel,
        name="gates",
        grid=(CTX // step,),
        out_shape=tuple(jax.ShapeDtypeStruct((CHL, TOK), BF16) for _ in range(4))
        + tuple(
            jax.ShapeDtypeStruct(s, F32)
            for s in ((EMB, ORDER), (1, ORDER), (ORDER, ORDER), (1, ORDER), (ORDER, TP * GRL))
        ),
        in_specs=[gates] * 4
        + [pl.BlockSpec((4, step, 4, 16, 256), lambda i: (0, i, 0, 0, 0)), fixed(CTX, 8, 256)],
        out_specs=(gates,) * 4
        + (fixed(EMB, ORDER), fixed(1, ORDER), fixed(ORDER, ORDER), fixed(1, ORDER), fixed(ORDER, TP * GRL)),
        compiler_params=pltpu.CompilerParams(vmem_limit_bytes=32 * 1024 * 1024),
        cost_estimate=pl.CostEstimate(flops=4_000_000, bytes_accessed=11_000_000, transcendentals=0),
    )(query, key, value, cot, back, summed)
    return mixed, g_query, g_key, g_value, o_w1, o_b1[0], o_w2, o_b2[0], o_w3


def solution(mesh):
    sharded = P("tp", "ctx")
    return jax.shard_map(
        on_device,
        mesh=mesh,
        in_specs=(sharded,) * 4 + (P("tp"), P("tp")) + (P(),) * 5,
        out_specs=(sharded,) * 4 + (P(),) * 5,
        check_vma=False,
    )
```

time: 462 us -> 97.2 us (0.21); the launches traced: 453 us -> 97 us
  waiting for transfers between devices: 145 us -> 0 us
  matrix products: 106 us -> 0 us
  Pallas kernels: 0 us -> 93.8 us
  blocking collectives: 84.9 us -> 0 us
  starting transfers between devices: 46.8 us -> 0 us
  local copies, waits for them, and re-layouts: 32.6 us -> 2.5 us
  other arithmetic: 22.8 us -> 0 us
  between operations: 15.1 us -> 0.73 us
    dot_general x44 -> x0, matrix products: 106 us -> none  [the longest x36 90.2 us: contract(): jnp.einsum(form, left, right, precision=TRANSFORM_MODE, preferred_element...]
    pallas_call x0 -> x2, Pallas kernels: none -> 93.8 us  [the longest x1 89.4 us: on_device(): pl.pallas_call(mixer_kernel, name='mixer', out_shape=(jax.ShapeDtypeStruc...]
    all_to_all x9 -> x0, waiting for transfers between devices: 79.8 us -> none  [the longest x1 16.1 us: on_device(): lax.all_to_all(mixed_own, 'ctx', split_axis=1, concat_axis=0, tiled=True)]
    psum x1 -> x0, blocking collectives: 69.4 us -> none  [on_device(): lax.psum((grad_one, bias_one, grad_two, bias_two, grad_three), ('ctx', 't...]
    psum x1 -> x0, waiting for transfers between devices: 65.3 us -> none  [on_device(): lax.psum((grad_one, bias_one, grad_two, bias_two, grad_three), ('ctx', 't...]
    all_to_all x9 -> x0, starting transfers between devices: 46.8 us -> none  [the longest x1 7.29 us: on_device(): lax.all_to_all(value_in, 'ctx', split_axis=0, concat_axis=1, tiled=True)]
    all_to_all x1 -> x0, blocking collectives: 15.6 us -> none  [on_device(): lax.all_to_all(filter_bf, 'ctx', split_axis=0, concat_axis=1, tiled=True)]
    convert_element_type x5 -> x0, other arithmetic: 9.11 us -> none  [the longest x1 3.76 us: owner_backward(): signal_grad = (back_part + bias_own[:, None] * grad_f).astype(jnp.bfloat16)]
  transfers between devices with their start and end apart: 10 -> 0, of which waited for: 7 -> 0; matrix products, arithmetic and copies ran while one was open for 23% -> 0% of each run, Pallas kernels for 0% -> 0%
where the time goes in v1:
time: 97.2 us; the launch traced here: 97 us
  Pallas kernels  93.8 us (97%)
  local copies, waits for them, and re-layouts  2.5 us (3%)
    pallas_call x1, Pallas kernels, on_device(): pl.pallas_call(mixer_kernel, name='mixer', out_shape=(jax.ShapeDtypeStruc...  89.4 us
    pallas_call x1, Pallas kernels, on_device(): pl.pallas_call(gate_kernel, name='gates', grid=(CTX // step,), out_shape=...  4.37 us
    unnamed x12, local copies, waits for them, and re-layouts  2.5 us

profile of v1, /device:TPU:1, one launch (start us, length us, event | category | flops | bytes accessed | tf_op | source)
XLA Modules:
  0.0 97.0 jit_solution(5925174160412189766)
XLA Ops:
  0.6 0.0 copy-start.1
  0.7 0.0 copy-start.2
  0.7 0.0 copy-start.3
  0.7 0.0 copy-start.4
  0.7 89.4 %mixer.1 = (bf16[4,16,4,16,256]{4,3,2,1,0:T(8,128)(2,1)}, f32[16,8,256]{2,1,0:T(8,128)}) custom-call(bf16[512,1024]{1,0:T(8,128)(2,1)} %query.3, bf16[512,1024]{1,0:T(8,128)(2,1)} %key.3, bf16[512,1024]{1,0:T(8,128)(2,1)} %value.3, bf16[512,1024]{1,0:T(8,128)(2,1)} %cot.3, f32[512]{0:T(512)} %skip.1, f32[1,32]{1,0:T(1,128)} %bitcast.5, f32[33,64]{1,0:T(8,128)} %w1.1, ...), custom_call_target="tpu_custom_call" | custom-call | flops 12000000000 | bytes 10000000 | tf_op jit(solution)/shard_map/mixer/pallas_call | solution.py:439
  90.1 0.0 copy-done.1
  90.1 0.0 copy-done.2
  90.1 0.0 copy-done.3
  90.1 0.0 copy-done.4
  90.1 0.0 copy-start
  90.1 1.6 %copy-done = bf16[4,16,4,16,256]{4,3,2,1,0:T(8,128)(2,1)S(1)} copy-done((bf16[4,16,4,16,256]{4,3,2,1,0:T(8,128)(2,1)S(1)}, bf16[4,16,4,16,256]{4,3,2,1,0:T(8,128)(2,1)}, u32[]{:S(2)}) %copy-start) | copy-done | bytes 2097176
  91.7 0.0 copy-start.5
  91.7 0.9 copy-done.5
  92.6 4.4 %gates.1 = (bf16[512,1024]{1,0:T(8,128)(2,1)}, bf16[512,1024]{1,0:T(8,128)(2,1)}, bf16[512,1024]{1,0:T(8,128)(2,1)}, bf16[512,1024]{1,0:T(8,128)(2,1)}, f32[33,6...) custom-call(bf16[512,1024]{1,0:T(8,128)(2,1)S(1)} %copy-done.1, ...), custom_call_target="tpu_custom_call" | custom-call | flops 4000000 | bytes 11000000 | tf_op jit(solution)/shard_map/gates/pallas_call | solution.py:469
Async XLA Ops:
  0.6 89.4 %copy-start.1 = (bf16[512,1024]{1,0:T(8,128)(2,1)S(1)}, bf16[512,1024]{1,0:T(8,128)(2,1)}, u32[]{:S(2)}) copy-start(bf16[512,1024]{1,0:T(8,128)(2,1)} %query.3) | copy-start | bytes 3145732
  0.7 89.4 %copy-start.2 = (bf16[512,1024]{1,0:T(8,128)(2,1)S(1)}, bf16[512,1024]{1,0:T(8,128)(2,1)}, u32[]{:S(2)}) copy-start(bf16[512,1024]{1,0:T(8,128)(2,1)} %key.3) | copy-start | bytes 3145732
  0.7 89.4 %copy-start.3 = (bf16[512,1024]{1,0:T(8,128)(2,1)S(1)}, bf16[512,1024]{1,0:T(8,128)(2,1)}, u32[]{:S(2)}) copy-start(bf16[512,1024]{1,0:T(8,128)(2,1)} %value.3) | copy-start | bytes 3145732
  0.7 89.4 %copy-start.4 = (bf16[512,1024]{1,0:T(8,128)(2,1)S(1)}, bf16[512,1024]{1,0:T(8,128)(2,1)}, u32[]{:S(2)}) copy-start(bf16[512,1024]{1,0:T(8,128)(2,1)} %cot.3) | copy-start | bytes 3145732
  90.1 1.6 %copy-start = (bf16[4,16,4,16,256]{4,3,2,1,0:T(8,128)(2,1)S(1)}, bf16[4,16,4,16,256]{4,3,2,1,0:T(8,128)(2,1)}, u32[]{:S(2)}) copy-start(bf16[4,16,4,16,256]{4,3,2,1,0:T(8,128)(2,1)} %get-tuple-element.20.back) | copy-start | bytes 6291460
  91.7 0.9 copy-start.5

commit v2 on v1

--- a/solution.py
+++ b/solution.py
@@ -180,6 +180,11 @@
     def push(rnd, j):
         remote(send.at[rnd, j], mine(rnd), S_IN + rnd, R_IN + rnd, "ctx", j).start()
 
+    def push_all(rnd):
+        @pl.loop(1, CTX)
+        def _(step):
+            push(rnd, ring(step))
+
     loads[0].wait()
     loads[1].wait()
     product(k_v, v_v, me, 0)
@@ -190,22 +195,12 @@
         product(k_v, v_v, ring(step), 0)
         push(0, ring(step))
 
-    @pl.loop(1, CTX)
-    def _(step):
-        push(1, ring(step))
-
     loads[2].wait()
     loads[3].wait()
-    product(q_v, g_v, me, 1)
-
-    @pl.loop(1, CTX)
-    def _(step):
-        product(q_v, g_v, ring(step), 1)
-        push(2, ring(step))
-
-    @pl.loop(1, CTX)
-    def _(step):
-        push(3, ring(step))
+
+    @pl.loop(0, CTX)
+    def _(j):
+        product(q_v, g_v, j, 1)
 
     own = [local(send.at[rnd, me], mine(rnd), L_IN + rnd) for rnd in range(4)]
     for c in own:
@@ -243,6 +238,7 @@
         remote(fsend.at[ring(step)], frecv.at[me], S_FIL, R_FIL, "ctx", ring(step)).start()
 
     frecv[me] = fsend[me]
+    push_all(2)
 
     for c in rest[1:]:
         c.wait()
@@ -308,23 +304,25 @@
         keep.start()
         return keep
 
-    kept = []
-    for g in range(2):
-        arrived(g)
-
+    def each_duo(*steps):
         @pl.loop(0, 4)
         def _(d):
-            forward(g, d, spec_s, g)
-            inverse(g, d, spec_s, g, 1.0)
-
-        kept.append(give(g))
-
-    for g in range(2):
-        arrived(2 + g)
+            for step in steps:
+                step(d)
+
+    def forward_signal(g):
+        return lambda d: forward(g, d, spec_s, g)
+
+    def inverse_signal(g):
+        return lambda d: inverse(g, d, spec_s, g, 1.0)
+
+    def inverse_grad(g):
+        return lambda d: inverse(2 + g, d, spec_g, g, -1.0)
+
+    def forward_grad(g):
         corr[g] = jnp.zeros((256, 256), F32)
 
-        @pl.loop(0, 4)
-        def _(d):
+        def step(d):
             forward(2 + g, d, spec_g, g)
             for pair in range(2):
                 s_re, s_im = spec_s[g, d, pair, :, 0:128], spec_s[g, d, pair, :, 128:256]
@@ -332,6 +330,21 @@
                 corr[g, :, 0:128] += g_re * s_re + g_im * s_im
                 corr[g, :, 128:256] += g_im * s_re - g_re * s_im
 
+        return step
+
+    arrived(0)
+    push_all(1)
+    each_duo(forward_signal(0), inverse_signal(0))
+    push_all(3)
+    kept = [give(0)]
+    arrived(2)
+    each_duo(forward_grad(0), inverse_grad(0))
+    kept.append(give(2))
+    arrived(1)
+    each_duo(forward_signal(1))
+    arrived(3)
+    each_duo(forward_grad(1))
+
     high, low = inverse_mid([corr[0], corr[1]])
     taps = dot(long[512:640, :], high) + dot(long[640:768, :], high) + dot(long[512:640, :], low)
     gsend[...] = taps.astype(BF16).astype(F32).reshape(CTX, 8, 256)
@@ -341,14 +354,8 @@
         remote(gsend.at[ring(step)], grecv.at[me], S_FG, R_FG, "ctx", ring(step)).start()
 
     grecv[me] = gsend[me]
-
-    for g in range(2):
-
-        @pl.loop(0, 4)
-        def _(d):
-            inverse(2 + g, d, spec_g, g, -1.0)
-
-        kept.append(give(2 + g))
+    each_duo(inverse_signal(1))
+    kept.append(give(1))
 
     landed(grecv.at[pl.ds(0, CTX - 1)], R_FG)
     got = jnp.stack([grecv[j, :, 128 * g : 128 * g + 128] for j in range(CTX) for g in range(2)], axis=0)
@@ -371,6 +378,8 @@
         remote(part.at[ring(step)], rs.at[me], S_RS, R_RS, "ctx", ring(step)).start()
 
     rs[me] = part[me]
+    each_duo(inverse_grad(1))
+    kept.append(give(3))
     landed(rs.at[pl.ds(0, CTX - 1)], R_RS)
     tpx[tp] = jnp.sum(rs[...], axis=0)
 
@@ -388,8 +397,9 @@
     landed(agx.at[pl.ds(0, CTX - 1)], R_AG)
     summed[...] = agx[...]
 
+    for c in kept:
+        c.wait()
     for rnd in range(4):
-        kept[rnd].wait()
         landed(back.at[rnd, pl.ds(0, CTX - 1)], R_OUT + rnd)
     for rnd in range(4):
         landed(send.at[rnd, pl.ds(0, CTX - 1)], S_IN + rnd)

time: 97.2 us -> 80.2 us (0.83)
  Pallas kernels: 93.8 us -> 76.8 us
    pallas_call x1, Pallas kernels: 89.4 us -> 72.4 us  [on_device(): pl.pallas_call(mixer_kernel, name='mixer', out_shape=(jax.ShapeDtypeStruc...]
where the time goes in v2:
time: 80.2 us; the launch traced here: 80 us
  Pallas kernels  76.8 us (96%)
  local copies, waits for them, and re-layouts  2.5 us (3%)
    pallas_call x1, Pallas kernels, on_device(): pl.pallas_call(mixer_kernel, name='mixer', out_shape=(jax.ShapeDtypeStruc...  72.4 us
    pallas_call x1, Pallas kernels, on_device(): pl.pallas_call(gate_kernel, name='gates', grid=(CTX // step,), out_shape=...  4.37 us
    unnamed x12, local copies, waits for them, and re-layouts  2.5 us

profile of v2, /device:TPU:1, one launch (start us, length us, event | category | flops | bytes accessed | tf_op | source)
XLA Modules:
  0.0 80.0 jit_solution(16017961438933491751)
XLA Ops:
  0.6 0.0 copy-start.1
  0.7 0.0 copy-start.2
  0.7 0.0 copy-start.3
  0.7 0.0 copy-start.4
  0.7 72.4 %mixer.1 = (bf16[4,16,4,16,256]{4,3,2,1,0:T(8,128)(2,1)}, f32[16,8,256]{2,1,0:T(8,128)}) custom-call(bf16[512,1024]{1,0:T(8,128)(2,1)} %query.3, bf16[512,1024]{1,0:T(8,128)(2,1)} %key.3, bf16[512,1024]{1,0:T(8,128)(2,1)} %value.3, bf16[512,1024]{1,0:T(8,128)(2,1)} %cot.3, f32[512]{0:T(512)} %skip.1, f32[1,32]{1,0:T(1,128)} %bitcast.5, f32[33,64]{1,0:T(8,128)} %w1.1, ...), custom_call_target="tpu_custom_call" | custom-call | flops 12000000000 | bytes 10000000 | tf_op jit(solution)/shard_map/mixer/pallas_call | solution.py:449
  73.1 0.0 copy-done.1
  73.1 0.0 copy-done.2
  73.1 0.0 copy-done.3
  73.1 0.0 copy-done.4
  73.1 0.0 copy-start
  73.2 1.6 %copy-done = bf16[4,16,4,16,256]{4,3,2,1,0:T(8,128)(2,1)S(1)} copy-done((bf16[4,16,4,16,256]{4,3,2,1,0:T(8,128)(2,1)S(1)}, bf16[4,16,4,16,256]{4,3,2,1,0:T(8,128)(2,1)}, u32[]{:S(2)}) %copy-start) | copy-done | bytes 2097176
  74.7 0.0 copy-start.5
  74.7 0.9 %copy-done.5 = f32[16,8,256]{2,1,0:T(8,128)S(1)} copy-done((f32[16,8,256]{2,1,0:T(8,128)S(1)}, f32[16,8,256]{2,1,0:T(8,128)}, u32[]{:S(2)}) %copy-start.5) | copy-done | bytes 131096
  75.6 4.4 %gates.1 = (bf16[512,1024]{1,0:T(8,128)(2,1)}, bf16[512,1024]{1,0:T(8,128)(2,1)}, bf16[512,1024]{1,0:T(8,128)(2,1)}, bf16[512,1024]{1,0:T(8,128)(2,1)}, f32[33,6...) custom-call(bf16[512,1024]{1,0:T(8,128)(2,1)S(1)} %copy-done.1, ...), custom_call_target="tpu_custom_call" | custom-call | flops 4000000 | bytes 11000000 | tf_op jit(solution)/shard_map/gates/pallas_call | solution.py:479
Async XLA Ops:
  0.6 72.5 %copy-start.1 = (bf16[512,1024]{1,0:T(8,128)(2,1)S(1)}, bf16[512,1024]{1,0:T(8,128)(2,1)}, u32[]{:S(2)}) copy-start(bf16[512,1024]{1,0:T(8,128)(2,1)} %query.3) | copy-start | bytes 3145732
  0.7 72.5 %copy-start.2 = (bf16[512,1024]{1,0:T(8,128)(2,1)S(1)}, bf16[512,1024]{1,0:T(8,128)(2,1)}, u32[]{:S(2)}) copy-start(bf16[512,1024]{1,0:T(8,128)(2,1)} %key.3) | copy-start | bytes 3145732
  0.7 72.5 %copy-start.3 = (bf16[512,1024]{1,0:T(8,128)(2,1)S(1)}, bf16[512,1024]{1,0:T(8,128)(2,1)}, u32[]{:S(2)}) copy-start(bf16[512,1024]{1,0:T(8,128)(2,1)} %value.3) | copy-start | bytes 3145732
  0.7 72.5 %copy-start.4 = (bf16[512,1024]{1,0:T(8,128)(2,1)S(1)}, bf16[512,1024]{1,0:T(8,128)(2,1)}, u32[]{:S(2)}) copy-start(bf16[512,1024]{1,0:T(8,128)(2,1)} %cot.3) | copy-start | bytes 3145732
  73.1 1.6 %copy-start = (bf16[4,16,4,16,256]{4,3,2,1,0:T(8,128)(2,1)S(1)}, bf16[4,16,4,16,256]{4,3,2,1,0:T(8,128)(2,1)}, u32[]{:S(2)}) copy-start(bf16[4,16,4,16,256]{4,3,2,1,0:T(8,128)(2,1)} %get-tuple-element.20.back) | copy-start | bytes 6291460
  74.7 0.9 %copy-start.5 = (f32[16,8,256]{2,1,0:T(8,128)S(1)}, f32[16,8,256]{2,1,0:T(8,128)}, u32[]{:S(2)}) copy-start(f32[16,8,256]{2,1,0:T(8,128)} %get-tuple-element.21.summed) | copy-start | bytes 393220

commit v3 on v2

--- a/solution.py
+++ b/solution.py
@@ -31,6 +31,7 @@
 ANY = pl.BlockSpec(memory_space=pl.ANY)
 VMEM = pl.BlockSpec(memory_space=pltpu.VMEM)
 SMEM = pl.BlockSpec(memory_space=pltpu.SMEM)
+HBM = pl.BlockSpec(memory_space=pltpu.HBM)
 
 PI_A = 3.140625
 PI_B = float(np.float32(math.floor((math.pi - PI_A) * 2.0**22) / 2.0**22))
@@ -116,22 +117,32 @@
 S_IN, R_IN, L_IN = 0, 4, 8
 S_OUT, R_OUT, L_OUT = 12, 16, 20
 S_FIL, R_FIL, S_FG, R_FG, S_RS, R_RS, S_TP, R_TP, S_AG, R_AG = range(24, 34)
-C_ARG, C_TAB = 34, 38
-N_SEM = 44
+C_ARG, C_TAB, C_SMALL = 34, 38, 43
+N_SEM = 49
 
 
 def mixer_kernel(
-    query, key, value, cot, skip, decay, w1, b1, w2, b2, w3, wide_h, thin_h, long_h, twid_h, feat_h,
+    query, key, value, cot, skip, decay_h, w1_h, b1_h, w2_h, b2_h, w3_h, wide_h, thin_h, long_h, twid_h, feat_h,
     back, summed,
-    q_v, k_v, v_v, g_v, wide, thin, long, twid, feat,
-    send, recv, spec_s, spec_g, spec_f, corr, out,
-    w1a, w2a, h1a, c1, s2, c2, dec, env, fsend, frecv, gsend, grecv, draw, dact, part, rs, tpx, agx, sem,
+    q_v, k_v, v_v, g_v, decay, w1, b1, w2, b2, w3, wide, thin, long, twid, feat,
+    send, recv, spec_s, spec_g, spec_f, corr, rows_f, out,
+    w1a, w2a, h1a, c1, s2, c2, dec, env, fsend, frecv, gsend, grecv, draw, dact, m_feat, m_out, part, rs, tpx, agx, sem,
 ):
     me = lax.axis_index("ctx")
     tp = lax.axis_index("tp")
 
     def ring(step):
         return lax.rem(me + step, CTX)
+
+    barrier = pltpu.get_barrier_semaphore()
+
+    @pl.loop(1, CTX)
+    def _(step):
+        pl.semaphore_signal(barrier, inc=1, device_id={"ctx": ring(step)}, device_id_type=MESH)
+
+    @pl.loop(1, TP)
+    def _(step):
+        pl.semaphore_signal(barrier, inc=1, device_id={"tp": lax.rem(tp + step, TP)}, device_id_type=MESH)
 
     def remote(src, dst, s, r, axis, j):
         return pltpu.make_async_remote_copy(
@@ -154,18 +165,14 @@
         local(long_h, long, C_TAB + 3),
         local(twid_h, twid, C_TAB + 4),
     ]
-    for c in rest:
+    small = [
+        local(a, b, C_SMALL + i)
+        for i, (a, b) in enumerate(
+            ((decay_h, decay), (w1_h, w1), (b1_h, b1), (w2_h, w2), (b2_h, b2), (w3_h, w3))
+        )
+    ]
+    for c in rest[:1] + small + rest[1:]:
         c.start()
-
-    barrier = pltpu.get_barrier_semaphore()
-
-    @pl.loop(1, CTX)
-    def _(step):
-        pl.semaphore_signal(barrier, inc=1, device_id={"ctx": ring(step)}, device_id_type=MESH)
-
-    @pl.loop(1, TP)
-    def _(step):
-        pl.semaphore_signal(barrier, inc=1, device_id={"tp": lax.rem(tp + step, TP)}, device_id_type=MESH)
 
     def product(left, right, j, kind):
         rows = pl.ds(pl.multiple_of(j * OWN, OWN), OWN)
@@ -202,11 +209,14 @@
     def _(j):
         product(q_v, g_v, j, 1)
 
+    push_all(2)
     own = [local(send.at[rnd, me], mine(rnd), L_IN + rnd) for rnd in range(4)]
     for c in own:
         c.start()
 
     rest[0].wait()
+    for c in small:
+        c.wait()
     feat[FROWS:, :] = jnp.zeros((64 - FROWS, TOK), F32)
     w1a[...] = jnp.zeros(w1a.shape, F32)
     w1a[0:EMB, :] = w1[...]
@@ -228,17 +238,14 @@
     rate = dot_full(dec[...], h1a[ORDER:, :], ((0,), (0,)))
     position = (me * TOK + lax.broadcasted_iota(jnp.int32, (GRL, TOK), 1)).astype(F32)
     env[...] = jnp.exp(-position * rate) * jnp.sqrt(2.0 * rate + 1.0 / SEQ)
-    tiles = rows_to_tiles((raw * env[...]).astype(BF16).astype(F32))
-    for j in range(CTX):
-        fsend[j, :, 0:128] = tiles[2 * j]
-        fsend[j, :, 128:256] = tiles[2 * j + 1]
+    fsend[...] = rows_to_tiles(raw * env[...]).reshape(CTX, 16, 128).astype(BF16)
 
     @pl.loop(1, CTX)
     def _(step):
         remote(fsend.at[ring(step)], frecv.at[me], S_FIL, R_FIL, "ctx", ring(step)).start()
 
     frecv[me] = fsend[me]
-    push_all(2)
+    push_all(1)
 
     for c in rest[1:]:
         c.wait()
@@ -262,7 +269,8 @@
         return split(jnp.concatenate([jnp.concatenate(res, axis=1), jnp.concatenate(ims, axis=1)], axis=0))
 
     landed(frecv.at[pl.ds(0, CTX - 1)], R_FIL)
-    taps = frecv[...].reshape(128, 256).astype(BF16)
+    taps = frecv[...].astype(F32).reshape(CTX, 2, 8, 128)
+    taps = jnp.concatenate([taps[:, g].reshape(128, 128) for g in range(2)], axis=1).astype(BF16)
     first = dot(thin[0:512, :], taps) + dot(thin[512:1024, :], taps)
     for g in range(2):
         spec_f[g] = forward_mid(first, g)
@@ -291,21 +299,30 @@
         scale = jnp.concatenate(
             [jnp.where(in_second, skip[base + 2 * pair + 1], skip[base + 2 * pair]) for pair in range(2)], axis=1
         )
-        out[rnd, d] = (y + scale * recv[rnd, d].astype(F32)).astype(BF16)
+        rows_f[d] = y + scale * recv[rnd, d].astype(F32)
+
+    def back_rows(rnd):
+        return back.at[rnd // 2, pl.ds(pl.multiple_of(me * OWN + rnd % 2 * 16, 16), 16), :]
 
     def give(rnd):
+        def turn(j):
+            block = pl.ds(pl.multiple_of(j * 16, 16), 16)
+            tiles = [rows_f[d, block, 128 * p : 128 * p + 128] for d in range(4) for p in range(2)]
+            out[rnd, j] = tiles_to_rows(jnp.stack(tiles, axis=0).reshape(16, 8, 128)).astype(BF16)
+
         @pl.loop(1, CTX)
         def _(step):
             j = ring(step)
-            src = out.at[rnd, :, pl.ds(pl.multiple_of(j * 16, 16), 16), :]
-            remote(src, back.at[rnd, me], S_OUT + rnd, R_OUT + rnd, "ctx", j).start()
-
-        keep = local(out.at[rnd, :, pl.ds(pl.multiple_of(me * 16, 16), 16), :], back.at[rnd, me], L_OUT + rnd)
+            turn(j)
+            remote(out.at[rnd, j], back_rows(rnd), S_OUT + rnd, R_OUT + rnd, "ctx", j).start()
+
+        turn(me)
+        keep = local(out.at[rnd, me], back_rows(rnd), L_OUT + rnd)
         keep.start()
         return keep
 
     def each_duo(*steps):
-        @pl.loop(0, 4)
+        @pl.loop(0, 4, unroll=4)
         def _(d):
             for step in steps:
                 step(d)
@@ -333,9 +350,8 @@
         return step
 
     arrived(0)
-    push_all(1)
+    push_all(3)
     each_duo(forward_signal(0), inverse_signal(0))
-    push_all(3)
     kept = [give(0)]
     arrived(2)
     each_duo(forward_grad(0), inverse_grad(0))
@@ -347,7 +363,9 @@
 
     high, low = inverse_mid([corr[0], corr[1]])
     taps = dot(long[512:640, :], high) + dot(long[640:768, :], high) + dot(long[512:640, :], low)
-    gsend[...] = taps.astype(BF16).astype(F32).reshape(CTX, 8, 256)
+    taps = taps.reshape(CTX, 1, 8, 256)
+    taps = jnp.concatenate([taps[..., 0:128], taps[..., 128:256]], axis=1)
+    gsend[...] = taps.reshape(CTX, 16, 128).astype(BF16)
 
     @pl.loop(1, CTX)
     def _(step):
@@ -358,20 +376,21 @@
     kept.append(give(1))
 
     landed(grecv.at[pl.ds(0, CTX - 1)], R_FG)
-    got = jnp.stack([grecv[j, :, 128 * g : 128 * g + 128] for j in range(CTX) for g in range(2)], axis=0)
+    got = grecv[...].astype(F32).reshape(GRL, 8, 128)
     draw[0:GRL, :] = tiles_to_rows(got) * (1.0 / math.sqrt(GSIZE * SEQ)) * env[...]
     draw[GRL:, :] = jnp.zeros((128 - GRL, TOK), F32)
     w3_own = pltpu.roll(w3[...], lax.rem(TP * GRL - tp * GRL, TP * GRL), 1)[:, 0:GRL]
     dact[0:ORDER, :] = dot_full(w3_own, draw[0:GRL, :], ((1,), (0,))) * c2[...]
     dact[ORDER:, :] = dot_full(w2[...], dact[0:ORDER, :], ((1,), (0,))) * c1[...]
-    g_feat = dot_full(feat[...], dact[...], ((1,), (1,)))
+    m_feat[...] = dot_full(feat[...], dact[...], ((1,), (1,)))
     g_hid = dot_full(h1a[0:ORDER, :], dact[...], ((1,), (1,)))
     g_out = dot_full(s2[...], draw[...], ((1,), (1,)))
-    g_out = pltpu.roll(jnp.concatenate([g_out, jnp.zeros((ORDER, 128), F32)], axis=1), tp * GRL, 1)
-    for i in range(8):
-        part[2 * i, :, 0:128] = g_feat[8 * i : 8 * i + 8, :]
-        part[2 * i, :, 128:256] = g_hid[8 * i : 8 * i + 8, :]
-        part[2 * i + 1] = g_out[8 * i : 8 * i + 8, :]
+    lane = lax.broadcasted_iota(jnp.int32, (ORDER, 128), 1)
+    m_out[...] = jnp.where(lane < ORDER, g_hid, pltpu.roll(g_out, ORDER, 1))
+    part[...] = jnp.zeros(part.shape, F32)
+    for q in range(CTX):
+        part[q, 0:4, :] = m_out[4 * q : 4 * q + 4, :]
+        part[q, 4:7, :] = m_feat[3 * q : 3 * q + 3, :]
 
     @pl.loop(1, CTX)
     def _(step):
@@ -388,22 +407,33 @@
         remote(tpx.at[tp], tpx.at[tp], S_TP, R_TP, "tp", lax.rem(tp + step, TP)).start()
 
     landed(tpx.at[pl.ds(0, TP - 1)], R_TP)
-    agx[me] = jnp.sum(tpx[...], axis=0)
+    agx[me, 0:8, :] = jnp.sum(tpx[...], axis=0)
+    row = lax.broadcasted_iota(jnp.int32, (8, 128), 0)
+    lane = lax.broadcasted_iota(jnp.int32, (8, 128), 1)
+    columns = jnp.zeros((8, 128), F32)
+    for k in range(TP):
+        piece = pltpu.roll(tpx[k], (GRL * (k % 4) - ORDER) % 128, 1)
+        if k >= 4:
+            piece = pltpu.roll(piece, 4, 0)
+        columns = jnp.where((lane // GRL == k % 4) & (row // 4 == k // 4), piece, columns)
+    agx[me, 8:16, :] = columns
 
     @pl.loop(1, CTX)
     def _(step):
         remote(agx.at[me], agx.at[me], S_AG, R_AG, "ctx", ring(step)).start()
 
     landed(agx.at[pl.ds(0, CTX - 1)], R_AG)
-    summed[...] = agx[...]
+    final = local(agx, summed, C_SMALL)
+    final.start()
+    kept.append(final)
 
     for c in kept:
         c.wait()
     for rnd in range(4):
-        landed(back.at[rnd, pl.ds(0, CTX - 1)], R_OUT + rnd)
+        landed(back.at[rnd // 2, pl.ds(0, 240), :], R_OUT + rnd)
     for rnd in range(4):
         landed(send.at[rnd, pl.ds(0, CTX - 1)], S_IN + rnd)
-        landed(out.at[rnd, :, pl.ds(0, 240), :], S_OUT + rnd)
+        landed(out.at[rnd, pl.ds(0, CTX - 1)], S_OUT + rnd)
     landed(fsend.at[pl.ds(0, CTX - 1)], S_FIL)
     landed(gsend.at[pl.ds(0, CTX - 1)], S_FG)
     landed(part.at[pl.ds(0, CTX - 1)], S_RS)
@@ -412,34 +442,59 @@
 
 
 def gate_kernel(
-    query, key, value, cot, back, summed, mixed, g_query, g_key, g_value, o_w1, o_b1, o_w2, o_b2, o_w3
+    query, key, value, cot, back, summed, mixed, g_query, g_key, g_value, o_w1, o_b1, o_w2, o_b2, o_w3,
+    inner, gates, results, sums, m_feat, sem_in, sem_gate, sem_out, sem_sum,
 ):
-    count = query.shape[0] // OWN
-    for j in range(count):
-        rows = slice(OWN * j, OWN * j + OWN)
-
-        def whole(kind):
-            tiles = [
-                back[2 * kind + p // 8, j, p % 8 // 2, :, 128 * (p % 2) : 128 * (p % 2) + 128] for p in range(16)
-            ]
-            return tiles_to_rows(jnp.stack(tiles, axis=0).astype(F32).reshape(OWN, 8, 128))
-
-        inner = whole(0)
-        mixed[rows, :] = (query[rows, :].astype(F32) * inner).astype(BF16)
-        g_query[rows, :] = (cot[rows, :].astype(F32) * inner).astype(BF16)
-        g_signal = whole(1)
-        g_key[rows, :] = (g_signal * value[rows, :].astype(F32)).astype(BF16)
-        g_value[rows, :] = (g_signal * key[rows, :].astype(F32)).astype(BF16)
-
-    @pl.when(pl.program_id(0) == 0)
-    def _():
-        feat = jnp.concatenate([summed[2 * i, :, 0:128] for i in range(8)], axis=0)
-        turned = pltpu.roll(feat, 64, 1)
-        o_w1[...] = turned[0:EMB, 0:ORDER]
-        o_b1[...] = turned[EMB : EMB + 1, 0:ORDER]
-        o_b2[...] = feat[EMB : EMB + 1, 0:ORDER]
-        o_w2[...] = jnp.concatenate([summed[2 * i, :, 128:256] for i in range(8)], axis=0)[:, 0:ORDER]
-        o_w3[...] = jnp.concatenate([summed[2 * i + 1] for i in range(8)], axis=0)
+    count = inner.shape[0]
+    height = CHL // count
+    fetch = [
+        [
+            pltpu.make_async_copy(back.at[kind, pl.ds(i * height, height), :], inner.at[i, kind], sem_in.at[i, kind])
+            for kind in range(2)
+        ]
+        for i in range(count)
+    ]
+    given = [
+        [
+            pltpu.make_async_copy(x.at[pl.ds(i * height, height), :], gates.at[i, k], sem_gate.at[i, k])
+            for k, x in enumerate((query, cot, value, key))
+        ]
+        for i in range(count)
+    ]
+    for i in range(count):
+        for kind in range(2):
+            for c in [fetch[i][kind]] + given[i][2 * kind : 2 * kind + 2]:
+                c.start()
+    load_sums = pltpu.make_async_copy(summed, sums, sem_sum)
+    load_sums.start()
+    stores = []
+    for i in range(count):
+        rows = slice(i * height, i * height + height)
+        for kind in range(2):
+            fetch[i][kind].wait()
+            for k in range(2):
+                given[i][2 * kind + k].wait()
+                results[2 * kind + k, rows, :] = gates[i, 2 * kind + k] * inner[i, kind]
+                target = (mixed, g_query, g_key, g_value)[2 * kind + k]
+                c = pltpu.make_async_copy(
+                    results.at[2 * kind + k, pl.ds(i * height, height), :],
+                    target.at[pl.ds(i * height, height), :],
+                    sem_out.at[i, 2 * kind + k],
+                )
+                c.start()
+                stores.append(c)
+    load_sums.wait()
+    for q in range(CTX):
+        m_feat[3 * q : 3 * q + 3, :] = sums[q, 4:7, :]
+        o_w2[4 * q : 4 * q + 4, :] = sums[q, 0:4, 0:ORDER]
+        o_w3[4 * q : 4 * q + 4, 0:128] = sums[q, 8:12, :]
+        o_w3[4 * q : 4 * q + 4, 128:256] = sums[q, 12:16, :]
+    turned = pltpu.roll(m_feat[...], ORDER, 1)
+    o_w1[...] = turned[0:EMB, 0:ORDER]
+    o_b1[...] = turned[EMB : EMB + 1, 0:ORDER]
+    o_b2[...] = m_feat[EMB : EMB + 1, 0:ORDER]
+    for c in stores:
+        c.wait()
 
 
 def on_device(query, key, value, cot, skip, decay, w1, b1, w2, b2, w3):
@@ -450,22 +505,23 @@
         mixer_kernel,
         name="mixer",
         out_shape=(
-            jax.ShapeDtypeStruct((4, CTX, 4, 16, 256), BF16),
-            jax.ShapeDtypeStruct((CTX, 8, 256), F32),
+            jax.ShapeDtypeStruct((2, CHL, TOK), BF16),
+            jax.ShapeDtypeStruct((CTX, 16, 128), F32),
         ),
-        in_specs=[ANY] * 4 + [SMEM] + [VMEM] * 6 + [ANY] * 5,
-        out_specs=(ANY, VMEM),
+        in_specs=[ANY] * 4 + [SMEM] + [ANY] * 11,
+        out_specs=(ANY, ANY),
         scratch_shapes=[
             *[b16(CHL, TOK) for _ in range(4)],
+            f32(1, GRL), f32(EMB, ORDER), f32(1, ORDER), f32(ORDER, ORDER), f32(1, ORDER), f32(ORDER, TP * GRL),
             b16(*wide.shape), b16(*thin.shape), b16(*long.shape), f32(*twid.shape), f32(64, TOK),
             b16(4, CTX, 4, 16, 256), b16(4, 4, 256, 256),
             f32(2, 4, 2, 256, 256), f32(2, 4, 2, 256, 256), f32(2, 256, 256), f32(2, 256, 256),
-            b16(4, 4, 256, 256),
+            f32(4, 256, 256), b16(4, CTX, 16, TOK),
             f32(FROWS, ORDER), f32(ORDER + 8, ORDER), f32(ORDER + 8, TOK), f32(ORDER, TOK), f32(ORDER, TOK),
             f32(ORDER, TOK), f32(8, GRL), f32(GRL, TOK),
-            f32(CTX, 8, 256), f32(CTX, 8, 256), f32(CTX, 8, 256), f32(CTX, 8, 256),
-            f32(128, TOK), f32(128, TOK),
-            f32(CTX, 8, 256), f32(CTX, 8, 256), f32(TP, 8, 256), f32(CTX, 8, 256),
+            *[b16(CTX, 16, 128) for _ in range(4)],
+            f32(128, TOK), f32(128, TOK), f32(ORDER, 128), f32(ORDER, 128),
+            f32(CTX, 8, 128), f32(CTX, 8, 128), f32(TP, 8, 128), f32(CTX, 16, 128),
             pltpu.SemaphoreType.DMA((N_SEM,)),
         ],
         compiler_params=pltpu.CompilerParams(
@@ -473,23 +529,22 @@
         ),
         cost_estimate=pl.CostEstimate(flops=12_000_000_000, bytes_accessed=10_000_000, transcendentals=200_000),
     )(query, key, value, cot, skip, decay[None], w1, b1[None], w2, b2[None], w3, wide, thin, long, twid, feat)
-    step = 2
-    gates = pl.BlockSpec((OWN * step, TOK), lambda i: (i, 0))
-    fixed = lambda *shape: pl.BlockSpec(shape, lambda i: (0,) * len(shape))
+    chunks = 4
     mixed, g_query, g_key, g_value, o_w1, o_b1, o_w2, o_b2, o_w3 = pl.pallas_call(
         gate_kernel,
         name="gates",
-        grid=(CTX // step,),
         out_shape=tuple(jax.ShapeDtypeStruct((CHL, TOK), BF16) for _ in range(4))
         + tuple(
             jax.ShapeDtypeStruct(s, F32)
             for s in ((EMB, ORDER), (1, ORDER), (ORDER, ORDER), (1, ORDER), (ORDER, TP * GRL))
         ),
-        in_specs=[gates] * 4
-        + [pl.BlockSpec((4, step, 4, 16, 256), lambda i: (0, i, 0, 0, 0)), fixed(CTX, 8, 256)],
-        out_specs=(gates,) * 4
-        + (fixed(EMB, ORDER), fixed(1, ORDER), fixed(ORDER, ORDER), fixed(1, ORDER), fixed(ORDER, TP * GRL)),
-        compiler_params=pltpu.CompilerParams(vmem_limit_bytes=32 * 1024 * 1024),
+        in_specs=[ANY] * 6,
+        out_specs=(ANY,) * 4 + (VMEM,) * 5,
+        scratch_shapes=[
+            b16(chunks, 2, CHL // chunks, TOK), b16(chunks, 4, CHL // chunks, TOK), b16(4, CHL, TOK), f32(CTX, 16, 128), f32(48, 128),
+            pltpu.SemaphoreType.DMA((chunks, 2)), pltpu.SemaphoreType.DMA((chunks, 4)), pltpu.SemaphoreType.DMA((chunks, 4)), pltpu.SemaphoreType.DMA,
+        ],
+        compiler_params=pltpu.CompilerParams(vmem_limit_bytes=63963136),
         cost_estimate=pl.CostEstimate(flops=4_000_000, bytes_accessed=11_000_000, transcendentals=0),
     )(query, key, value, cot, back, summed)
     return mixed, g_query, g_key, g_value, o_w1, o_b1[0], o_w2, o_b2[0], o_w3

time: 80.2 us -> 75.4 us (0.940)
  local copies, waits for them, and re-layouts: 2.5 us -> 0 us
  Pallas kernels: 76.8 us -> 74.5 us
    pallas_call x1, Pallas kernels: 72.4 us -> 69.3 us  [on_device(): pl.pallas_call(mixer_kernel, name='mixer', out_shape=(jax.ShapeDtypeStruc...]
    unnamed x12 -> x0, local copies, waits for them, and re-layouts: 2.5 us -> none
where the time goes in v3:
time: 75.4 us; the launch traced here: 75.3 us
  Pallas kernels  74.5 us (99%)
  between operations  0.81 us (1%)
    pallas_call x1, Pallas kernels, on_device(): pl.pallas_call(mixer_kernel, name='mixer', out_shape=(jax.ShapeDtypeStruc...  69.3 us
    pallas_call x1, Pallas kernels, on_device(): pl.pallas_call(gate_kernel, name='gates', out_shape=tuple((jax.ShapeDtype...  5.12 us

profile of v3, /device:TPU:1, one launch (start us, length us, event | category | flops | bytes accessed | tf_op | source)
XLA Modules:
  0.0 75.3 jit_solution(14237601888390267452)
XLA Ops:
  0.6 69.3 %mixer.1 = (bf16[2,512,1024]{2,1,0:T(8,128)(2,1)}, f32[16,16,128]{2,1,0:T(8,128)}) custom-call(bf16[512,1024]{1,0:T(8,128)(2,1)} %query.3, bf16[512,1024]{1,0:T(8,128)(2,1)} %key.3, bf16[512,1024]{1,0:T(8,128)(2,1)} %value.3, bf16[512,1024]{1,0:T(8,128)(2,1)} %cot.3, f32[512]{0:T(512)} %skip.1, f32[1,32]{1,0:T(1,128)} %bitcast.5, f32[33,64]{1,0:T(8,128)} %w1_h.1, ...), custom_call_target="tpu_custom_call" | custom-call | flops 12000000000 | bytes 10000000 | tf_op jit(solution)/shard_map/mixer/pallas_call | solution.py:504
  70.0 5.1 %gates.1 = (bf16[512,1024]{1,0:T(8,128)(2,1)}, bf16[512,1024]{1,0:T(8,128)(2,1)}, bf16[512,1024]{1,0:T(8,128)(2,1)}, bf16[512,1024]{1,0:T(8,128)(2,1)}, f32[33,6...) custom-call(bf16[512,1024]{1,0:T(8,128)(2,1)} %query.3, ...), custom_call_target="tpu_custom_call" | custom-call | flops 4000000 | bytes 11000000 | tf_op jit(solution)/shard_map/gates/pallas_call | solution.py:533

commit v4 on v3

--- a/solution.py
+++ b/solution.py
@@ -423,9 +423,7 @@
         remote(agx.at[me], agx.at[me], S_AG, R_AG, "ctx", ring(step)).start()
 
     landed(agx.at[pl.ds(0, CTX - 1)], R_AG)
-    final = local(agx, summed, C_SMALL)
-    final.start()
-    kept.append(final)
+    summed[...] = agx[...]
 
     for c in kept:
         c.wait()
@@ -443,38 +441,16 @@
 
 def gate_kernel(
     query, key, value, cot, back, summed, mixed, g_query, g_key, g_value, o_w1, o_b1, o_w2, o_b2, o_w3,
-    inner, gates, results, sums, m_feat, sem_in, sem_gate, sem_out, sem_sum,
+    results, m_feat, sem_out,
 ):
-    count = inner.shape[0]
+    count = sem_out.shape[0]
     height = CHL // count
-    fetch = [
-        [
-            pltpu.make_async_copy(back.at[kind, pl.ds(i * height, height), :], inner.at[i, kind], sem_in.at[i, kind])
-            for kind in range(2)
-        ]
-        for i in range(count)
-    ]
-    given = [
-        [
-            pltpu.make_async_copy(x.at[pl.ds(i * height, height), :], gates.at[i, k], sem_gate.at[i, k])
-            for k, x in enumerate((query, cot, value, key))
-        ]
-        for i in range(count)
-    ]
-    for i in range(count):
-        for kind in range(2):
-            for c in [fetch[i][kind]] + given[i][2 * kind : 2 * kind + 2]:
-                c.start()
-    load_sums = pltpu.make_async_copy(summed, sums, sem_sum)
-    load_sums.start()
     stores = []
     for i in range(count):
         rows = slice(i * height, i * height + height)
-        for kind in range(2):
-            fetch[i][kind].wait()
-            for k in range(2):
-                given[i][2 * kind + k].wait()
-                results[2 * kind + k, rows, :] = gates[i, 2 * kind + k] * inner[i, kind]
+        for kind, factors in enumerate(((query, cot), (value, key))):
+            for k, factor in enumerate(factors):
+                results[2 * kind + k, rows, :] = factor[rows, :] * back[kind, rows, :]
                 target = (mixed, g_query, g_key, g_value)[2 * kind + k]
                 c = pltpu.make_async_copy(
                     results.at[2 * kind + k, pl.ds(i * height, height), :],
@@ -483,12 +459,11 @@
                 )
                 c.start()
                 stores.append(c)
-    load_sums.wait()
     for q in range(CTX):
-        m_feat[3 * q : 3 * q + 3, :] = sums[q, 4:7, :]
-        o_w2[4 * q : 4 * q + 4, :] = sums[q, 0:4, 0:ORDER]
-        o_w3[4 * q : 4 * q + 4, 0:128] = sums[q, 8:12, :]
-        o_w3[4 * q : 4 * q + 4, 128:256] = sums[q, 12:16, :]
+        m_feat[3 * q : 3 * q + 3, :] = summed[q, 4:7, :]
+        o_w2[4 * q : 4 * q + 4, :] = summed[q, 0:4, 0:ORDER]
+        o_w3[4 * q : 4 * q + 4, 0:128] = summed[q, 8:12, :]
+        o_w3[4 * q : 4 * q + 4, 128:256] = summed[q, 12:16, :]
     turned = pltpu.roll(m_feat[...], ORDER, 1)
     o_w1[...] = turned[0:EMB, 0:ORDER]
     o_b1[...] = turned[EMB : EMB + 1, 0:ORDER]
@@ -505,11 +480,11 @@
         mixer_kernel,
         name="mixer",
         out_shape=(
-            jax.ShapeDtypeStruct((2, CHL, TOK), BF16),
-            jax.ShapeDtypeStruct((CTX, 16, 128), F32),
+            pltpu.VMEM((2, CHL, TOK), BF16),
+            pltpu.VMEM((CTX, 16, 128), F32),
         ),
         in_specs=[ANY] * 4 + [SMEM] + [ANY] * 11,
-        out_specs=(ANY, ANY),
+        out_specs=(VMEM, VMEM),
         scratch_shapes=[
             *[b16(CHL, TOK) for _ in range(4)],
             f32(1, GRL), f32(EMB, ORDER), f32(1, ORDER), f32(ORDER, ORDER), f32(1, ORDER), f32(ORDER, TP * GRL),
@@ -538,13 +513,12 @@
             jax.ShapeDtypeStruct(s, F32)
             for s in ((EMB, ORDER), (1, ORDER), (ORDER, ORDER), (1, ORDER), (ORDER, TP * GRL))
         ),
-        in_specs=[ANY] * 6,
+        in_specs=[VMEM] * 6,
         out_specs=(ANY,) * 4 + (VMEM,) * 5,
         scratch_shapes=[
-            b16(chunks, 2, CHL // chunks, TOK), b16(chunks, 4, CHL // chunks, TOK), b16(4, CHL, TOK), f32(CTX, 16, 128), f32(48, 128),
-            pltpu.SemaphoreType.DMA((chunks, 2)), pltpu.SemaphoreType.DMA((chunks, 4)), pltpu.SemaphoreType.DMA((chunks, 4)), pltpu.SemaphoreType.DMA,
+            b16(4, CHL, TOK), f32(48, 128), pltpu.SemaphoreType.DMA((chunks, 4)),
         ],
-        compiler_params=pltpu.CompilerParams(vmem_limit_bytes=63963136),
+        compiler_params=pltpu.CompilerParams(vmem_limit_bytes=32 * 1024 * 1024),
         cost_estimate=pl.CostEstimate(flops=4_000_000, bytes_accessed=11_000_000, transcendentals=0),
     )(query, key, value, cot, back, summed)
     return mixed, g_query, g_key, g_value, o_w1, o_b1[0], o_w2, o_b2[0], o_w3

time: 75.4 us -> 72.6 us (0.963)
  Pallas kernels: 74.5 us -> 71.5 us
    pallas_call x1, Pallas kernels: 5.12 us -> 2.83 us  [on_device(): pl.pallas_call(gate_kernel, name='gates', out_shape=tuple((jax.ShapeDtype...]
where the time goes in v4:
time: 72.6 us; the launch traced here: 72.4 us
  Pallas kernels  71.5 us (98%)
  between operations  0.88 us (1%)
    pallas_call x1, Pallas kernels, on_device(): pl.pallas_call(mixer_kernel, name='mixer', out_shape=(pltpu.VMEM((2, CHL,...  68.7 us
    pallas_call x1, Pallas kernels, on_device(): pl.pallas_call(gate_kernel, name='gates', out_shape=tuple((jax.ShapeDtype...  2.83 us

profile of v4, /device:TPU:1, one launch (start us, length us, event | category | flops | bytes accessed | tf_op | source)
XLA Modules:
  0.0 72.4 jit_solution(1778558528701873570)
XLA Ops:
  0.6 0.0 copy-start
  0.7 0.0 copy-start.1
  0.7 0.0 copy-start.2
  0.7 0.0 copy-start.3
  0.7 68.7 %mixer.1 = (bf16[2,512,1024]{2,1,0:T(8,128)(2,1)S(1)}, f32[16,16,128]{2,1,0:T(8,128)S(1)}) custom-call(bf16[512,1024]{1,0:T(8,128)(2,1)} %query.3, bf16[512,1024]{1,0:T(8,128)(2,1)} %key.3, bf16[512,1024]{1,0:T(8,128)(2,1)} %value.3, bf16[512,1024]{1,0:T(8,128)(2,1)} %cot.3, f32[512]{0:T(512)} %skip.1, f32[1,32]{1,0:T(1,128)} %bitcast.5, f32[33,64]{1,0:T(8,128)} %w1_h.1, ...), custom_call_target="tpu_custom_call" | custom-call | flops 12000000000 | bytes 10000000 | tf_op jit(solution)/shard_map/mixer/pallas_call | solution.py:479
  69.4 0.0 copy-done
  69.4 0.0 copy-done.1
  69.4 0.0 copy-done.2
  69.4 0.0 copy-done.3
  69.5 2.8 %gates.1 = (bf16[512,1024]{1,0:T(8,128)(2,1)}, bf16[512,1024]{1,0:T(8,128)(2,1)}, bf16[512,1024]{1,0:T(8,128)(2,1)}, bf16[512,1024]{1,0:T(8,128)(2,1)}, f32[33,6...) custom-call(bf16[512,1024]{1,0:T(8,128)(2,1)S(1)} %copy-done, ...), custom_call_target="tpu_custom_call" | custom-call | flops 4000000 | bytes 11000000 | tf_op jit(solution)/shard_map/gates/pallas_call | solution.py:508
Async XLA Ops:
  0.6 68.8 %copy-start = (bf16[512,1024]{1,0:T(8,128)(2,1)S(1)}, bf16[512,1024]{1,0:T(8,128)(2,1)}, u32[]{:S(2)}) copy-start(bf16[512,1024]{1,0:T(8,128)(2,1)} %query.3) | copy-start | bytes 3145732
  0.7 68.8 %copy-start.1 = (bf16[512,1024]{1,0:T(8,128)(2,1)S(1)}, bf16[512,1024]{1,0:T(8,128)(2,1)}, u32[]{:S(2)}) copy-start(bf16[512,1024]{1,0:T(8,128)(2,1)} %key.3) | copy-start | bytes 3145732
  0.7 68.8 %copy-start.2 = (bf16[512,1024]{1,0:T(8,128)(2,1)S(1)}, bf16[512,1024]{1,0:T(8,128)(2,1)}, u32[]{:S(2)}) copy-start(bf16[512,1024]{1,0:T(8,128)(2,1)} %value.3) | copy-start | bytes 3145732
  0.7 68.8 %copy-start.3 = (bf16[512,1024]{1,0:T(8,128)(2,1)S(1)}, bf16[512,1024]{1,0:T(8,128)(2,1)}, u32[]{:S(2)}) copy-start(bf16[512,1024]{1,0:T(8,128)(2,1)} %cot.3) | copy-start | bytes 3145732

commit v5 on v4

--- a/solution.py
+++ b/solution.py
@@ -88,6 +88,12 @@
     )
 
 
+def dot_three(left, right, dims):
+    return lax.dot_general(
+        left, right, (dims, ((), ())), precision=lax.Precision.HIGH, preferred_element_type=F32
+    )
+
+
 def split(x):
     high = x.astype(BF16)
     return high, (x - high.astype(F32)).astype(BF16)
@@ -116,7 +122,7 @@
 
 S_IN, R_IN, L_IN = 0, 4, 8
 S_OUT, R_OUT, L_OUT = 12, 16, 20
-S_FIL, R_FIL, S_FG, R_FG, S_RS, R_RS, S_TP, R_TP, S_AG, R_AG = range(24, 34)
+S_FIL, R_FIL, S_FG, R_FG, S_RS, R_RS, S_CX, R_CX, S_AG, R_AG = range(24, 34)
 C_ARG, C_TAB, C_SMALL = 34, 38, 43
 N_SEM = 49
 
@@ -126,7 +132,7 @@
     back, summed,
     q_v, k_v, v_v, g_v, decay, w1, b1, w2, b2, w3, wide, thin, long, twid, feat,
     send, recv, spec_s, spec_g, spec_f, corr, rows_f, out,
-    w1a, w2a, h1a, c1, s2, c2, dec, env, fsend, frecv, gsend, grecv, draw, dact, m_feat, m_out, part, rs, tpx, agx, sem,
+    w1a, w2a, h1a, c1, s2, c2, dec, env, fsend, frecv, gsend, grecv, draw, dact, m_feat, part, eighths, cx, agx, sem,
 ):
     me = lax.axis_index("ctx")
     tp = lax.axis_index("tp")
@@ -304,22 +310,24 @@
     def back_rows(rnd):
         return back.at[rnd // 2, pl.ds(pl.multiple_of(me * OWN + rnd % 2 * 16, 16), 16), :]
 
-    def give(rnd):
-        def turn(j):
+    def turn_all(rnd):
+        @pl.loop(0, CTX)
+        def _(j):
             block = pl.ds(pl.multiple_of(j * 16, 16), 16)
             tiles = [rows_f[d, block, 128 * p : 128 * p + 128] for d in range(4) for p in range(2)]
             out[rnd, j] = tiles_to_rows(jnp.stack(tiles, axis=0).reshape(16, 8, 128)).astype(BF16)
 
+    kept = []
+
+    def send_out(rnd):
         @pl.loop(1, CTX)
         def _(step):
             j = ring(step)
-            turn(j)
             remote(out.at[rnd, j], back_rows(rnd), S_OUT + rnd, R_OUT + rnd, "ctx", j).start()
 
-        turn(me)
         keep = local(out.at[rnd, me], back_rows(rnd), L_OUT + rnd)
         keep.start()
-        return keep
+        kept.append(keep)
 
     def each_duo(*steps):
         @pl.loop(0, 4, unroll=4)
@@ -352,10 +360,12 @@
     arrived(0)
     push_all(3)
     each_duo(forward_signal(0), inverse_signal(0))
-    kept = [give(0)]
+    turn_all(0)
+    send_out(0)
     arrived(2)
     each_duo(forward_grad(0), inverse_grad(0))
-    kept.append(give(2))
+    turn_all(2)
+    send_out(2)
     arrived(1)
     each_duo(forward_signal(1))
     arrived(3)
@@ -373,56 +383,49 @@
 
     grecv[me] = gsend[me]
     each_duo(inverse_signal(1))
-    kept.append(give(1))
+    turn_all(1)
 
     landed(grecv.at[pl.ds(0, CTX - 1)], R_FG)
     got = grecv[...].astype(F32).reshape(GRL, 8, 128)
     draw[0:GRL, :] = tiles_to_rows(got) * (1.0 / math.sqrt(GSIZE * SEQ)) * env[...]
     draw[GRL:, :] = jnp.zeros((128 - GRL, TOK), F32)
     w3_own = pltpu.roll(w3[...], lax.rem(TP * GRL - tp * GRL, TP * GRL), 1)[:, 0:GRL]
-    dact[0:ORDER, :] = dot_full(w3_own, draw[0:GRL, :], ((1,), (0,))) * c2[...]
-    dact[ORDER:, :] = dot_full(w2[...], dact[0:ORDER, :], ((1,), (0,))) * c1[...]
-    m_feat[...] = dot_full(feat[...], dact[...], ((1,), (1,)))
-    g_hid = dot_full(h1a[0:ORDER, :], dact[...], ((1,), (1,)))
-    g_out = dot_full(s2[...], draw[...], ((1,), (1,)))
-    lane = lax.broadcasted_iota(jnp.int32, (ORDER, 128), 1)
-    m_out[...] = jnp.where(lane < ORDER, g_hid, pltpu.roll(g_out, ORDER, 1))
-    part[...] = jnp.zeros(part.shape, F32)
-    for q in range(CTX):
-        part[q, 0:4, :] = m_out[4 * q : 4 * q + 4, :]
-        part[q, 4:7, :] = m_feat[3 * q : 3 * q + 3, :]
+    dact[0:ORDER, :] = dot_three(w3_own, draw[0:GRL, :], ((1,), (0,))) * c2[...]
+    dact[ORDER:, :] = dot_three(w2[...], dact[0:ORDER, :], ((1,), (0,))) * c1[...]
+    m_feat[...] = dot_three(feat[...], dact[...], ((1,), (1,)))
+    m_feat[EMB + 1 : EMB + 2, :] = pltpu.roll(m_feat[...], ORDER, 1)[EMB : EMB + 1, :]
+    g_hid = dot_three(h1a[0:ORDER, :], dact[...], ((1,), (1,)))
+    g_out = dot_three(s2[...], draw[...], ((1,), (1,)))
+    lane = lax.broadcasted_iota(jnp.int32, (8, 128), 1)
+    for k in range(TP):
+        part[k] = jnp.where(lane < ORDER, g_hid[8 * k : 8 * k + 8, :], m_feat[5 * k : 5 * k + 8, :])
+    cx[me, 8:24, :] = sum(pltpu.roll(g_out[16 * i : 16 * i + 16, :], GRL * i, 1) for i in range(4))
+
+    @pl.loop(1, TP)
+    def _(step):
+        k = lax.rem(tp + step, TP)
+        remote(part.at[k], eighths.at[tp], S_RS, R_RS, "tp", k).start()
+
+    eighths[tp] = part[tp]
+    send_out(1)
+    each_duo(inverse_grad(1))
+    turn_all(3)
+    landed(eighths.at[pl.ds(0, TP - 1)], R_RS)
+    cx[me, 0:8, :] = jnp.sum(eighths[...], axis=0)
 
     @pl.loop(1, CTX)
     def _(step):
-        remote(part.at[ring(step)], rs.at[me], S_RS, R_RS, "ctx", ring(step)).start()
-
-    rs[me] = part[me]
-    each_duo(inverse_grad(1))
-    kept.append(give(3))
-    landed(rs.at[pl.ds(0, CTX - 1)], R_RS)
-    tpx[tp] = jnp.sum(rs[...], axis=0)
+        remote(cx.at[me], cx.at[me], S_CX, R_CX, "ctx", ring(step)).start()
+
+    send_out(3)
+    landed(cx.at[pl.ds(0, CTX - 1)], R_CX)
+    agx[tp] = jnp.sum(cx[...], axis=0)
 
     @pl.loop(1, TP)
     def _(step):
-        remote(tpx.at[tp], tpx.at[tp], S_TP, R_TP, "tp", lax.rem(tp + step, TP)).start()
-
-    landed(tpx.at[pl.ds(0, TP - 1)], R_TP)
-    agx[me, 0:8, :] = jnp.sum(tpx[...], axis=0)
-    row = lax.broadcasted_iota(jnp.int32, (8, 128), 0)
-    lane = lax.broadcasted_iota(jnp.int32, (8, 128), 1)
-    columns = jnp.zeros((8, 128), F32)
-    for k in range(TP):
-        piece = pltpu.roll(tpx[k], (GRL * (k % 4) - ORDER) % 128, 1)
-        if k >= 4:
-            piece = pltpu.roll(piece, 4, 0)
-        columns = jnp.where((lane // GRL == k % 4) & (row // 4 == k // 4), piece, columns)
-    agx[me, 8:16, :] = columns
-
-    @pl.loop(1, CTX)
-    def _(step):
-        remote(agx.at[me], agx.at[me], S_AG, R_AG, "ctx", ring(step)).start()
-
-    landed(agx.at[pl.ds(0, CTX - 1)], R_AG)
+        remote(agx.at[tp], agx.at[tp], S_AG, R_AG, "tp", lax.rem(tp + step, TP)).start()
+
+    landed(agx.at[pl.ds(0, TP - 1)], R_AG)
     summed[...] = agx[...]
 
     for c in kept:
@@ -434,9 +437,9 @@
         landed(out.at[rnd, pl.ds(0, CTX - 1)], S_OUT + rnd)
     landed(fsend.at[pl.ds(0, CTX - 1)], S_FIL)
     landed(gsend.at[pl.ds(0, CTX - 1)], S_FG)
-    landed(part.at[pl.ds(0, CTX - 1)], S_RS)
-    landed(tpx.at[pl.ds(0, TP - 1)], S_TP)
-    landed(agx.at[pl.ds(0, CTX - 1)], S_AG)
+    landed(part.at[pl.ds(0, TP - 1)], S_RS)
+    landed(cx.at[pl.ds(0, CTX - 1)], S_CX)
+    landed(agx.at[pl.ds(0, TP - 1)], S_AG)
 
 
 def gate_kernel(
@@ -459,15 +462,21 @@
                 )
                 c.start()
                 stores.append(c)
-    for q in range(CTX):
-        m_feat[3 * q : 3 * q + 3, :] = summed[q, 4:7, :]
-        o_w2[4 * q : 4 * q + 4, :] = summed[q, 0:4, 0:ORDER]
-        o_w3[4 * q : 4 * q + 4, 0:128] = summed[q, 8:12, :]
-        o_w3[4 * q : 4 * q + 4, 128:256] = summed[q, 12:16, :]
-    turned = pltpu.roll(m_feat[...], ORDER, 1)
-    o_w1[...] = turned[0:EMB, 0:ORDER]
-    o_b1[...] = turned[EMB : EMB + 1, 0:ORDER]
-    o_b2[...] = m_feat[EMB : EMB + 1, 0:ORDER]
+    for k in range(TP):
+        m_feat[5 * k : 5 * k + 5, :] = summed[k, 0:5, :]
+        o_w2[8 * k : 8 * k + 8, :] = summed[k, 0:8, 0:ORDER]
+    lane = lax.broadcasted_iota(jnp.int32, (16, 128), 1) // GRL
+    for half in range(2):
+        for i in range(4):
+            block = jnp.zeros((16, 128), F32)
+            for k in range(4):
+                turned = pltpu.roll(summed[4 * half + k, 8:24, :], GRL * (k - i) % 128, 1)
+                block = jnp.where(lane == k, turned, block)
+            o_w3[16 * i : 16 * i + 16, 128 * half : 128 * half + 128] = block
+    feat = pltpu.roll(m_feat[...], ORDER, 1)
+    o_w1[...] = feat[0:EMB, 0:ORDER]
+    o_b1[...] = feat[EMB : EMB + 1, 0:ORDER]
+    o_b2[...] = feat[EMB + 1 : EMB + 2, 0:ORDER]
     for c in stores:
         c.wait()
 
@@ -481,7 +490,7 @@
         name="mixer",
         out_shape=(
             pltpu.VMEM((2, CHL, TOK), BF16),
-            pltpu.VMEM((CTX, 16, 128), F32),
+            pltpu.VMEM((TP, 24, 128), F32),
         ),
         in_specs=[ANY] * 4 + [SMEM] + [ANY] * 11,
         out_specs=(VMEM, VMEM),
@@ -495,8 +504,8 @@
             f32(FROWS, ORDER), f32(ORDER + 8, ORDER), f32(ORDER + 8, TOK), f32(ORDER, TOK), f32(ORDER, TOK),
             f32(ORDER, TOK), f32(8, GRL), f32(GRL, TOK),
             *[b16(CTX, 16, 128) for _ in range(4)],
-            f32(128, TOK), f32(128, TOK), f32(ORDER, 128), f32(ORDER, 128),
-            f32(CTX, 8, 128), f32(CTX, 8, 128), f32(TP, 8, 128), f32(CTX, 16, 128),
+            f32(128, TOK), f32(128, TOK), f32(ORDER, 128),
+            f32(TP, 8, 128), f32(TP, 8, 128), f32(CTX, 24, 128), f32(TP, 24, 128),
             pltpu.SemaphoreType.DMA((N_SEM,)),
         ],
         compiler_params=pltpu.CompilerParams(
@@ -516,7 +525,7 @@
         in_specs=[VMEM] * 6,
         out_specs=(ANY,) * 4 + (VMEM,) * 5,
         scratch_shapes=[
-            b16(4, CHL, TOK), f32(48, 128), pltpu.SemaphoreType.DMA((chunks, 4)),
+            b16(4, CHL, TOK), f32(FROWS, 128), pltpu.SemaphoreType.DMA((chunks, 4)),
         ],
         compiler_params=pltpu.CompilerParams(vmem_limit_bytes=32 * 1024 * 1024),
         cost_estimate=pl.CostEstimate(flops=4_000_000, bytes_accessed=11_000_000, transcendentals=0),

time: 72.6 us -> 70.1 us (0.966)
  Pallas kernels: 71.5 us -> 68.9 us
    pallas_call x1, Pallas kernels: 68.7 us -> 66 us  [on_device(): pl.pallas_call(mixer_kernel, name='mixer', out_shape=(pltpu.VMEM((2, CHL,...]
where the time goes in v5:
time: 70.1 us; the launch traced here: 69.8 us
  Pallas kernels  68.9 us (98%)
  between operations  0.88 us (1%)
    pallas_call x1, Pallas kernels, on_device(): pl.pallas_call(mixer_kernel, name='mixer', out_shape=(pltpu.VMEM((2, CHL,...  66 us
    pallas_call x1, Pallas kernels, on_device(): pl.pallas_call(gate_kernel, name='gates', out_shape=tuple((jax.ShapeDtype...  2.86 us

profile of v5, /device:TPU:1, one launch (start us, length us, event | category | flops | bytes accessed | tf_op | source)
XLA Modules:
  0.0 69.8 jit_solution(17723521614813952788)
XLA Ops:
  0.6 0.0 copy-start
  0.7 0.0 copy-start.1
  0.7 0.0 copy-start.2
  0.7 0.0 copy-start.3
  0.7 66.0 %mixer.1 = (bf16[2,512,1024]{2,1,0:T(8,128)(2,1)S(1)}, f32[8,24,128]{2,1,0:T(8,128)S(1)}) custom-call(bf16[512,1024]{1,0:T(8,128)(2,1)} %query.3, bf16[512,1024]{1,0:T(8,128)(2,1)} %key.3, bf16[512,1024]{1,0:T(8,128)(2,1)} %value.3, bf16[512,1024]{1,0:T(8,128)(2,1)} %cot.3, f32[512]{0:T(512)} %skip.1, f32[1,32]{1,0:T(1,128)} %bitcast.5, f32[33,64]{1,0:T(8,128)} %w1_h.1, ...), custom_call_target="tpu_custom_call" | custom-call | flops 12000000000 | bytes 10000000 | tf_op jit(solution)/shard_map/mixer/pallas_call | solution.py:488
  66.7 0.0 copy-done
  66.7 0.0 copy-done.1
  66.7 0.0 copy-done.2
  66.8 0.0 copy-done.3
  66.8 2.9 %gates.1 = (bf16[512,1024]{1,0:T(8,128)(2,1)}, bf16[512,1024]{1,0:T(8,128)(2,1)}, bf16[512,1024]{1,0:T(8,128)(2,1)}, bf16[512,1024]{1,0:T(8,128)(2,1)}, f32[33,6...) custom-call(bf16[512,1024]{1,0:T(8,128)(2,1)S(1)} %copy-done, ...), custom_call_target="tpu_custom_call" | custom-call | flops 4000000 | bytes 11000000 | tf_op jit(solution)/shard_map/gates/pallas_call | solution.py:517
Async XLA Ops:
  0.6 66.1 %copy-start = (bf16[512,1024]{1,0:T(8,128)(2,1)S(1)}, bf16[512,1024]{1,0:T(8,128)(2,1)}, u32[]{:S(2)}) copy-start(bf16[512,1024]{1,0:T(8,128)(2,1)} %query.3) | copy-start | bytes 3145732
  0.7 66.1 %copy-start.1 = (bf16[512,1024]{1,0:T(8,128)(2,1)S(1)}, bf16[512,1024]{1,0:T(8,128)(2,1)}, u32[]{:S(2)}) copy-start(bf16[512,1024]{1,0:T(8,128)(2,1)} %key.3) | copy-start | bytes 3145732
  0.7 66.1 %copy-start.2 = (bf16[512,1024]{1,0:T(8,128)(2,1)S(1)}, bf16[512,1024]{1,0:T(8,128)(2,1)}, u32[]{:S(2)}) copy-start(bf16[512,1024]{1,0:T(8,128)(2,1)} %value.3) | copy-start | bytes 3145732
  0.7 66.1 %copy-start.3 = (bf16[512,1024]{1,0:T(8,128)(2,1)S(1)}, bf16[512,1024]{1,0:T(8,128)(2,1)}, u32[]{:S(2)}) copy-start(bf16[512,1024]{1,0:T(8,128)(2,1)} %cot.3) | copy-start | bytes 3145732

commit v6 on v5

--- a/solution.py
+++ b/solution.py
@@ -365,8 +365,8 @@
     arrived(2)
     each_duo(forward_grad(0), inverse_grad(0))
     turn_all(2)
+    arrived(1)
     send_out(2)
-    arrived(1)
     each_duo(forward_signal(1))
     arrived(3)
     each_duo(forward_grad(1))
@@ -395,11 +395,9 @@
     m_feat[...] = dot_three(feat[...], dact[...], ((1,), (1,)))
     m_feat[EMB + 1 : EMB + 2, :] = pltpu.roll(m_feat[...], ORDER, 1)[EMB : EMB + 1, :]
     g_hid = dot_three(h1a[0:ORDER, :], dact[...], ((1,), (1,)))
-    g_out = dot_three(s2[...], draw[...], ((1,), (1,)))
     lane = lax.broadcasted_iota(jnp.int32, (8, 128), 1)
     for k in range(TP):
         part[k] = jnp.where(lane < ORDER, g_hid[8 * k : 8 * k + 8, :], m_feat[5 * k : 5 * k + 8, :])
-    cx[me, 8:24, :] = sum(pltpu.roll(g_out[16 * i : 16 * i + 16, :], GRL * i, 1) for i in range(4))
 
     @pl.loop(1, TP)
     def _(step):
@@ -407,9 +405,10 @@
         remote(part.at[k], eighths.at[tp], S_RS, R_RS, "tp", k).start()
 
     eighths[tp] = part[tp]
+    g_out = dot_three(s2[...], draw[...], ((1,), (1,)))
+    cx[me, 8:24, :] = sum(pltpu.roll(g_out[16 * i : 16 * i + 16, :], GRL * i, 1) for i in range(4))
     send_out(1)
     each_duo(inverse_grad(1))
-    turn_all(3)
     landed(eighths.at[pl.ds(0, TP - 1)], R_RS)
     cx[me, 0:8, :] = jnp.sum(eighths[...], axis=0)
 
@@ -417,6 +416,7 @@
     def _(step):
         remote(cx.at[me], cx.at[me], S_CX, R_CX, "ctx", ring(step)).start()
 
+    turn_all(3)
     send_out(3)
     landed(cx.at[pl.ds(0, CTX - 1)], R_CX)
     agx[tp] = jnp.sum(cx[...], axis=0)

time: 70.1 us -> 70.8 us (level)
  Pallas kernels: 68.9 us -> 69.7 us
    pallas_call x1, Pallas kernels: 66 us -> 66.8 us  [on_device(): pl.pallas_call(mixer_kernel, name='mixer', out_shape=(pltpu.VMEM((2, CHL,...]
where the time goes in v6:
time: 70.8 us; the launch traced here: 70.6 us
  Pallas kernels  69.7 us (98%)
  between operations  0.88 us (1%)
    pallas_call x1, Pallas kernels, on_device(): pl.pallas_call(mixer_kernel, name='mixer', out_shape=(pltpu.VMEM((2, CHL,...  66.8 us
    pallas_call x1, Pallas kernels, on_device(): pl.pallas_call(gate_kernel, name='gates', out_shape=tuple((jax.ShapeDtype...  2.86 us

profile of v6, /device:TPU:1, one launch (start us, length us, event | category | flops | bytes accessed | tf_op | source)
XLA Modules:
  0.0 70.6 jit_solution(15992781743967788145)
XLA Ops:
  0.6 0.0 copy-start
  0.7 0.0 copy-start.1
  0.7 0.0 copy-start.2
  0.7 0.0 copy-start.3
  0.7 66.8 %mixer.1 = (bf16[2,512,1024]{2,1,0:T(8,128)(2,1)S(1)}, f32[8,24,128]{2,1,0:T(8,128)S(1)}) custom-call(bf16[512,1024]{1,0:T(8,128)(2,1)} %query.3, bf16[512,1024]{1,0:T(8,128)(2,1)} %key.3, bf16[512,1024]{1,0:T(8,128)(2,1)} %value.3, bf16[512,1024]{1,0:T(8,128)(2,1)} %cot.3, f32[512]{0:T(512)} %skip.1, f32[1,32]{1,0:T(1,128)} %bitcast.5, f32[33,64]{1,0:T(8,128)} %w1_h.1, ...), custom_call_target="tpu_custom_call" | custom-call | flops 12000000000 | bytes 10000000 | tf_op jit(solution)/shard_map/mixer/pallas_call | solution.py:488
  67.5 0.0 copy-done
  67.5 0.0 copy-done.1
  67.5 0.0 copy-done.2
  67.5 0.0 copy-done.3
  67.5 2.9 %gates.1 = (bf16[512,1024]{1,0:T(8,128)(2,1)}, bf16[512,1024]{1,0:T(8,128)(2,1)}, bf16[512,1024]{1,0:T(8,128)(2,1)}, bf16[512,1024]{1,0:T(8,128)(2,1)}, f32[33,6...) custom-call(bf16[512,1024]{1,0:T(8,128)(2,1)S(1)} %copy-done, ...), custom_call_target="tpu_custom_call" | custom-call | flops 4000000 | bytes 11000000 | tf_op jit(solution)/shard_map/gates/pallas_call | solution.py:517
Async XLA Ops:
  0.6 66.9 %copy-start = (bf16[512,1024]{1,0:T(8,128)(2,1)S(1)}, bf16[512,1024]{1,0:T(8,128)(2,1)}, u32[]{:S(2)}) copy-start(bf16[512,1024]{1,0:T(8,128)(2,1)} %query.3) | copy-start | bytes 3145732
  0.7 66.9 %copy-start.1 = (bf16[512,1024]{1,0:T(8,128)(2,1)S(1)}, bf16[512,1024]{1,0:T(8,128)(2,1)}, u32[]{:S(2)}) copy-start(bf16[512,1024]{1,0:T(8,128)(2,1)} %key.3) | copy-start | bytes 3145732
  0.7 66.9 %copy-start.2 = (bf16[512,1024]{1,0:T(8,128)(2,1)S(1)}, bf16[512,1024]{1,0:T(8,128)(2,1)}, u32[]{:S(2)}) copy-start(bf16[512,1024]{1,0:T(8,128)(2,1)} %value.3) | copy-start | bytes 3145732
  0.7 66.9 %copy-start.3 = (bf16[512,1024]{1,0:T(8,128)(2,1)S(1)}, bf16[512,1024]{1,0:T(8,128)(2,1)}, u32[]{:S(2)}) copy-start(bf16[512,1024]{1,0:T(8,128)(2,1)} %cot.3) | copy-start | bytes 3145732
